TPU v7x, 256 devices: a whole 4x4x8 slice. The times are simulated.
256 devices in a mesh: tile: 64 (over z, x, core), wp: 4 (over y).
Axes of the slice: x: 4, y: 4, z: 8, core: 2. Of those that a mesh axis runs over, the one named last changes fastest.
Arguments:
- visibilities: float32 [65536, 2, 128], P(('tile', 'wp')), may hold values from -6 to 6
- vis_weight: float32 [65536, 128], P(('tile', 'wp')), may hold values from 0.2 to 5
- cell_index: int32 [65536, 128], P(('tile', 'wp')), may hold values from 0 to 4095
- tap_offsets: int32 [65536, 128], P(('tile', 'wp')), may hold values from 0 to 255
- routes: int32 [65536, 1], P(('tile', 'wp')), may hold values from 0 to 255; in each aligned block of 256 rows (0 to 255, 256 to 511, ...) at most 2 rows name the same one
- patch_index: int32 [65536], P(('tile', 'wp')), may hold values from 0 to 255
- kernel: float32 [16, 8], replicated, may hold values from 0.1 to 1
Outputs:
- uv_grid: float32 [4, 64, 2, 1024, 1024], P('wp', 'tile')
Inputs may be any that keep to these rules, and one draw needn't show every extreme that they name: `routes`: the 256 blocks of one device name no value more than 2 times, a bound that some block reaches.
All inputs are finite; a program needn't handle non-finite values.
Results may differ from a plain program's by a relative error of at most 0.0003.
Values sent between devices are 32-bit elements; how exact they have to be, the bound alone decides.
A program may use at most 192 MiB of HBM per device.

v0:
```python
import jax
import jax.numpy as jnp
from jax import lax
from jax.sharding import PartitionSpec as P

TCOLS = 8
SUB = 64
KW = 8
OVER = 16
TILE = 1024


highest = lax.Precision.HIGHEST


def shifted(block, axis, distance):
    devices = range(lax.axis_size(axis))
    route = [(i - distance, i) for i in devices if i - distance in devices]
    return lax.ppermute(block, axis, route)


def kernel_taps(level_index, kernel):
    level_ids = lax.broadcasted_iota(
        jnp.int32, level_index.shape + (kernel.shape[0],), level_index.ndim
    )
    one_hot = jnp.where(level_index[..., None] == level_ids, 1.0, 0.0).astype(jnp.float32)
    return jnp.einsum("bro,ok->brk", one_hot, kernel, precision=highest)


def spread_matrix(first_cell, taps):
    extent = SUB + KW
    places = lax.broadcasted_iota(jnp.int32, first_cell.shape + (extent,), first_cell.ndim)
    matrix = jnp.zeros(first_cell.shape + (extent,), jnp.float32)
    for tap_index in range(KW):
        matrix = matrix + jnp.where(
            places == first_cell[..., None] + tap_index, taps[..., tap_index : tap_index + 1], 0.0
        )
    return matrix


def unfold_edges(patches):
    leading = patches.shape[:-2]
    block_count = patches.shape[-2]
    padding_keep = [(0, 0)] * len(leading)
    core_part = patches[..., :SUB].reshape(leading + (block_count * SUB,))
    core_part = jnp.pad(core_part, padding_keep + [(0, KW)])
    edge_part = jnp.pad(patches[..., SUB:], padding_keep + [(0, 0), (0, SUB - KW)])
    edge_part = edge_part.reshape(leading + (block_count * SUB,))
    edge_part = jnp.pad(edge_part, padding_keep + [(SUB, 0)])[..., : block_count * SUB + KW]
    return core_part + edge_part


def shards(visibilities, vis_weight, cell_index, tap_offsets, routes, patch_index, kernel):
    blocks = visibilities.shape[0]
    tile_count = lax.axis_size("tile")
    plane_count = lax.axis_size("wp")
    peer_count = tile_count * plane_count
    capacity = max(2, 2 * blocks // peer_count)
    levels = OVER * OVER
    target = routes[:, 0]
    earlier = lax.broadcasted_iota(jnp.int32, (blocks, blocks), 1) < lax.broadcasted_iota(
        jnp.int32, (blocks, blocks), 0
    )
    matches = (target[:, None] == target[None, :]) & earlier
    order_in = jnp.sum(matches.astype(jnp.int32), axis=1)
    slot_index = target * capacity + order_in

    def bucket(values):
        buffer = jnp.zeros((peer_count * capacity,) + values.shape[1:], values.dtype)
        buffer = buffer.at[slot_index].set(values)
        return buffer.reshape((tile_count, plane_count, capacity) + values.shape[1:])

    float_part = visibilities * vis_weight[:, None, :]
    int_part = (cell_index * levels + tap_offsets)[:, None, :]
    sent_float = bucket(float_part)
    sent_ints = bucket(int_part)
    sent_patch = bucket(patch_index)
    arrived = (
        lax.all_to_all(
            lax.all_to_all(sent_float, "tile", split_axis=0, concat_axis=0, tiled=True),
            "wp",
            split_axis=1,
            concat_axis=1,
            tiled=True,
        ),
        lax.all_to_all(
            lax.all_to_all(sent_ints, "tile", split_axis=0, concat_axis=0, tiled=True),
            "wp",
            split_axis=1,
            concat_axis=1,
            tiled=True,
        ),
        lax.all_to_all(
            lax.all_to_all(sent_patch, "tile", split_axis=0, concat_axis=0, tiled=True),
            "wp",
            split_axis=1,
            concat_axis=1,
            tiled=True,
        ),
    )
    got_float, got_ints, got_patch = arrived
    slot_total = peer_count * capacity
    got_float = got_float.reshape((slot_total,) + got_float.shape[3:])
    got_ints = got_ints.reshape((slot_total,) + got_ints.shape[3:])
    got_patch = got_patch.reshape((slot_total,))
    got_cells = got_ints[:, 0] // levels
    got_offsets = got_ints[:, 0] % levels
    patches_across = TILE // SUB
    extent = SUB + KW
    batch_size = min(128, slot_total)
    patch_ids = lax.broadcasted_iota(jnp.int32, (1, patches_across * patches_across), 1)
    patch_list = []
    for first_slot in range(0, slot_total, batch_size):
        last_slot = first_slot + batch_size
        scaled = got_float[first_slot:last_slot]
        batch_cells = got_cells[first_slot:last_slot]
        batch_offsets = got_offsets[first_slot:last_slot]
        rows_along_u = spread_matrix(batch_cells // SUB, kernel_taps(batch_offsets // OVER, kernel))
        rows_along_v = spread_matrix(batch_cells % SUB, kernel_taps(batch_offsets % OVER, kernel))
        weighted = rows_along_u[:, None, :, :] * scaled[:, :, :, None]
        patches = jnp.einsum("bcru,brv->bcuv", weighted, rows_along_v, precision=highest)
        patch_list.append(patches.reshape(batch_size, -1))
    all_patches = jnp.concatenate(patch_list, axis=0)
    chosen = jnp.where(got_patch[:, None] == patch_ids, 1.0, 0.0).astype(jnp.float32)
    accum = jnp.einsum("bs,bx->sx", chosen, all_patches, precision=highest)
    patch_grid = accum.reshape(patches_across, patches_across, 2, extent, extent)
    along_v = unfold_edges(jnp.transpose(patch_grid, (2, 0, 3, 1, 4)))
    along_u = unfold_edges(jnp.transpose(along_v, (0, 3, 1, 2)))
    full_tile = jnp.transpose(along_u, (0, 2, 1))
    tile_place = lax.axis_index("tile")
    leftmost = tile_place % TCOLS == 0
    right_edge = jnp.swapaxes(full_tile[:, :TILE, TILE:], 1, 2)
    from_left = shifted(right_edge, "tile", 1)
    from_left = jnp.where(leftmost, 0.0, from_left)
    lower_edge = full_tile[:, TILE:, :TILE]
    from_above = shifted(lower_edge, "tile", TCOLS)
    corner_edge = full_tile[:, TILE:, TILE:]
    from_corner = shifted(corner_edge, "tile", TCOLS + 1)
    from_corner = jnp.where(leftmost, 0.0, from_corner)
    own_tile = full_tile[:, :TILE, :TILE]
    own_tile = own_tile.at[:, :, :KW].add(jnp.swapaxes(from_left, 1, 2))
    own_tile = own_tile.at[:, :KW, :].add(from_above)
    own_tile = own_tile.at[:, :KW, :KW].add(from_corner)
    return own_tile.reshape(1, 1, 2, TILE, TILE)


def solution(mesh):
    in_specs = (
        P(("tile", "wp"), None, None),
        P(("tile", "wp"), None),
        P(("tile", "wp"), None),
        P(("tile", "wp"), None),
        P(("tile", "wp"), None),
        P(("tile", "wp")),
        P(),
    )
    out_specs = P("wp", "tile", None, None, None)
    return jax.shard_map(shards, mesh=mesh, in_specs=in_specs, out_specs=out_specs, check_vma=False)
```

profile of v0, /device:TPU:8, one launch (start us, length us, event | category | flops | bytes accessed | tf_op | source)
XLA Modules:
  0.0 488.4 jit_solution(7850530664655946711)
XLA Ops:
  0.0 0.9 convert_reduce_fusion
  1.6 1.6 scatter_custom_fusion
  3.4 1.1 copy.151
  4.5 11.9 %all-to-all-start = ((s32[64,4,2]{1,2,0:T(2,128)}), s32[64,4,2]{1,2,0:T(2,128)S(1)}, u32[]{:S(2)}, u32[]{:S(2)}) async-start(s32[64,4,2]{1,2,0:T(2,128)} %copy.151), calls=%async_computation | async-start | bytes 131072 | tf_op jit(solution)/shard_map/all_to_all | solution.py:94
  16.4 2.3 scatter_custom_fusion.1
  18.7 7.7 %all-to-all-done = s32[64,4,2]{1,2,0:T(2,128)S(1)} async-done(((s32[64,4,2]{1,2,0:T(2,128)}), s32[64,4,2]{1,2,0:T(2,128)S(1)}, u32[]{:S(2)}, u32[]{:S(2)}) %all-to-all-start) | async-done | bytes 2080 | tf_op jit(solution)/shard_map/all_to_all | solution.py:94
  26.4 4.6 all-to-all-start.2
  31.8 12.2 %all-to-all-done.2 = s32[64,4,2,1,128]{4,2,1,3,0:T(2,128)S(1)} async-done(((s32[64,4,2,1,128]{4,2,1,3,0:T(2,128)}), s32[64,4,2,1,128]{4,2,1,3,0:T(2,128)S(1)}, u32[]{:S(2)}, u32[]{:S(2)}) %all-to-all-start.2) | async-done | bytes 262176 | tf_op jit(solution)/shard_map/all_to_all | solution.py:87
  44.0 4.9 %all-to-all-start.1 = ((s32[4,1,128]{2,1,0:T(1,128)}), s32[4,1,128]{2,1,0:T(1,128)S(1)}, u32[]{:S(2)}, u32[]{:S(2)}) async-start(s32[4,1,128]{2,1,0:T(1,128)} %reshape.471), calls=%async_computation.1 | async-start | bytes 4096 | tf_op jit(solution)/shard_map/all_to_all | solution.py:93
  49.0 0.8 copy.155
  49.7 2.9 all-to-all-done.1
  52.6 5.0 %all-to-all-start.3 = ((s32[64,4,2,1,128]{4,2,0,3,1:T(2,128)}), s32[64,4,2,1,128]{4,2,0,3,1:T(2,128)S(1)}, u32[]{:S(2)}, u32[]{:S(2)}) async-start(s32[64,4,2,1,128]{4,2,0,3,1:T(2,128)} %copy.155), calls=%async_computation.3 | async-start | bytes 524288 | tf_op jit(solution)/shard_map/all_to_all | solution.py:86
  57.6 1.1 broadcast_multiply_fusion
  58.7 0.9 broadcast_in_dim.676
  59.6 24.1 %scatter_fusion = f32[512,2,128]{2,1,0:T(2,128)} fusion(f32[512,2,128]{2,1,0:T(2,128)} %broadcast_in_dim.676, s32[256]{0:T(256)S(1)} %bitcast.228, f32[256,2,128]{2,1,0:T(2,128)S(1)} %broadcast_multiply_fusion), kind=kCustom, calls=%fused_computation.2 | custom fusion | bytes 787456 | tf_op jit(solution)/shard_map/scatter | solution.py:70
  85.2 5.1 %all-to-all-start.4 = ((f32[64,4,2,2,128]{4,3,2,1,0:T(2,128)}), f32[64,4,2,2,128]{4,3,2,1,0:T(2,128)S(1)}, u32[]{:S(2)}, u32[]{:S(2)}) async-start(f32[64,4,2,2,128]{4,3,2,1,0:T(2,128)} %bitcast.15), calls=%async_computation.4 | async-start | bytes 1048576 | tf_op jit(solution)/shard_map/all_to_all | solution.py:80
  92.5 0.8 fusion.164
  93.3 1.1 fusion.262
  95.5 0.8 broadcast_add_fusion.55
  97.9 0.7 fusion.158
  99.0 0.8 fusion.170
  101.4 11.9 %select_add_fusion.2 = f32[128,128,72]{1,2,0:T(8,128)} fusion(f32[128,128]{1,0:T(8,128)S(1)} %bitcast.184, s32[128,128]{1,0:T(8,128)S(1)} %get-tuple-element.183, f32[128,128]{1,0:T(8,128)S(1)} %bitcast.185, s32[128,128]{1,0:T(8,128)S(1)} %get-tuple-element.179, f32[128,128]{1,0:T(8,128)S(1)} %bitcast.186, s32[128,128]{1,0:T(8,128)S(1)} %get-tuple-element.180, ...), kind=kLoop, calls=%fused_computation.119 | loop fusion | flops 27131904 | bytes 5767168 | tf_op jit(solution)/shard_map/add | solution.py:35
  113.2 11.6 %select_add_fusion = f32[128,128,72]{1,2,0:T(8,128)} fusion(f32[128,128]{1,0:T(8,128)S(1)} %bitcast.176, s32[128,128]{1,0:T(8,128)S(1)} %get-tuple-element.207, f32[128,128]{1,0:T(8,128)S(1)} %bitcast.177, s32[128,128]{1,0:T(8,128)S(1)} %get-tuple-element.203, f32[128,128]{1,0:T(8,128)S(1)} %bitcast.178, s32[128,128]{1,0:T(8,128)S(1)} %get-tuple-element.204, ...), kind=kLoop, calls=%fused_computation.51 | loop fusion | flops 27131904 | bytes 5767168 | tf_op jit(solution)/shard_map/add | solution.py:35
  124.9 11.7 %select_add_fusion.1 = f32[128,128,72]{1,2,0:T(8,128)} fusion(f32[128,128]{1,0:T(8,128)S(1)} %bitcast.160, s32[128,128]{1,0:T(8,128)S(1)} %get-tuple-element.195, f32[128,128]{1,0:T(8,128)S(1)} %bitcast.161, s32[128,128]{1,0:T(8,128)S(1)} %get-tuple-element.191, f32[128,128]{1,0:T(8,128)S(1)} %bitcast.162, s32[128,128]{1,0:T(8,128)S(1)} %get-tuple-element.192, ...), kind=kLoop, calls=%fused_computation.85 | loop fusion | flops 27131904 | bytes 5767168 | tf_op jit(solution)/shard_map/add | solution.py:35
  136.6 0.8 fusion.160
  137.3 12.1 %select_add_fusion.3 = f32[128,128,72]{1,2,0:T(8,128)} fusion(f32[128,128]{1,0:T(8,128)S(1)} %bitcast.168, s32[128,128]{1,0:T(8,128)S(1)} %get-tuple-element.220, f32[128,128]{1,0:T(8,128)S(1)} %bitcast.169, s32[128,128]{1,0:T(8,128)S(1)} %get-tuple-element.224, f32[128,128]{1,0:T(8,128)S(1)} %bitcast.170, s32[128,128]{1,0:T(8,128)S(1)} %get-tuple-element.223, ...), kind=kLoop, calls=%fused_computation.153 | loop fusion | flops 27131904 | bytes 5767168 | tf_op jit(solution)/shard_map/add | solution.py:35
  149.4 1.0 copy.157
  150.4 4.8 all-to-all-start.5
  155.2 0.8 broadcast_add_fusion.30
  156.0 1.1 fusion.264
  157.1 6.5 %all-to-all-done.5 = f32[64,4,2,2,128]{4,3,2,0,1:T(2,128)S(1)} async-done(((f32[64,4,2,2,128]{4,3,2,0,1:T(2,128)}), f32[64,4,2,2,128]{4,3,2,0,1:T(2,128)S(1)}, u32[]{:S(2)}, u32[]{:S(2)}) %all-to-all-start.5) | async-done | bytes 524320 | tf_op jit(solution)/shard_map/all_to_all | solution.py:79
  164.5 17.6 %fusion.12 = f32[128,2,72,72]{3,2,1,0:T(8,128)} fusion(f32[128,2,128]{2,1,0:T(2,128)S(1)} %copy.162, f32[128,128,72]{1,2,0:T(8,128)} %select_add_fusion.2, f32[128,128]{1,0:T(8,128)} %bitcast.208, s32[128,128]{1,0:T(8,128)S(1)} %get-tuple-element.177, f32[128,128]{1,0:T(8,128)} %bitcast.209, s32[128,128]{1,0:T(8,128)S(1)} %get-tuple-element.173, ...), kind=kOutput, calls=%fused_computation.18 | convolution fusion | flops 2067922944 | bytes 11206656 | tf_op jit(solution)/shard_map/bcru,brv->bcuv/dot_general | solution.py:121
  182.1 8.5 %copy.163 = f32[128,2,72,72]{0,3,2,1:T(8,128)} copy(f32[128,2,72,72]{3,2,1,0:T(8,128)} %fusion.12) | data formatting | bytes 10616832 | tf_op jit(solution)/shard_map/bcru,brv->bcuv/dot_general | solution.py:121
  190.6 17.4 %fusion.8 = f32[128,2,72,72]{3,2,1,0:T(8,128)} fusion(f32[128,2,128]{2,1,0:T(2,128)S(1)} %copy.168, f32[128,128,72]{1,2,0:T(8,128)} %select_add_fusion, f32[128,128]{1,0:T(8,128)S(1)} %bitcast.200, s32[128,128]{1,0:T(8,128)S(1)} %get-tuple-element.201, f32[128,128]{1,0:T(8,128)S(1)} %bitcast.201, s32[128,128]{1,0:T(8,128)S(1)} %get-tuple-element.197, ...), kind=kOutput, calls=%fused_computation.14 | convolution fusion | flops 2067922944 | bytes 11206656 | tf_op jit(solution)/shard_map/bcru,brv->bcuv/dot_general | solution.py:121
  208.0 8.5 %copy.169 = f32[128,2,72,72]{0,3,2,1:T(8,128)} copy(f32[128,2,72,72]{3,2,1,0:T(8,128)} %fusion.8) | data formatting | bytes 10616832 | tf_op jit(solution)/shard_map/bcru,brv->bcuv/dot_general | solution.py:121
  216.6 17.5 %fusion.10 = f32[128,2,72,72]{3,2,1,0:T(8,128)} fusion(f32[128,2,128]{2,1,0:T(2,128)S(1)} %copy.165, f32[128,128,72]{1,2,0:T(8,128)} %select_add_fusion.1, f32[128,128]{1,0:T(8,128)S(1)} %bitcast.216, s32[128,128]{1,0:T(8,128)S(1)} %get-tuple-element.214, f32[128,128]{1,0:T(8,128)S(1)} %bitcast.217, s32[128,128]{1,0:T(8,128)S(1)} %get-tuple-element.218, ...), kind=kOutput, calls=%fused_computation.16 | convolution fusion | flops 2067922944 | bytes 11206656 | tf_op jit(solution)/shard_map/bcru,brv->bcuv/dot_general | solution.py:121
  234.2 8.5 %copy.166 = f32[128,2,72,72]{0,3,2,1:T(8,128)} copy(f32[128,2,72,72]{3,2,1,0:T(8,128)} %fusion.10) | data formatting | bytes 10616832 | tf_op jit(solution)/shard_map/bcru,brv->bcuv/dot_general | solution.py:121
  242.7 17.6 %fusion.14 = f32[128,2,72,72]{3,2,1,0:T(8,128)} fusion(f32[128,2,128]{2,1,0:T(2,128)S(1)} %copy.159, f32[128,128,72]{1,2,0:T(8,128)} %select_add_fusion.3, f32[128,128]{1,0:T(8,128)S(1)} %bitcast.192, s32[128,128]{1,0:T(8,128)S(1)} %copy-done.8, f32[128,128]{1,0:T(8,128)S(1)} %bitcast.193, s32[128,128]{1,0:T(8,128)S(1)} %copy-done.4, ...), kind=kOutput, calls=%fused_computation.20 | convolution fusion | flops 2067922944 | bytes 11206656 | tf_op jit(solution)/shard_map/bcru,brv->bcuv/dot_general | solution.py:121
  260.3 8.4 %copy.160 = f32[128,2,72,72]{0,3,2,1:T(8,128)} copy(f32[128,2,72,72]{3,2,1,0:T(8,128)} %fusion.14) | data formatting | bytes 10616832 | tf_op jit(solution)/shard_map/bcru,brv->bcuv/dot_general | solution.py:121
  268.7 31.7 %fusion = f32[256,10368]{1,0:T(8,128)} fusion(f32[128,10368]{0,1:T(8,128)} %bitcast.150, f32[128,10368]{0,1:T(8,128)} %bitcast.151, f32[128,10368]{0,1:T(8,128)} %bitcast.149, f32[128,10368]{0,1:T(8,128)} %bitcast.152, s32[512]{0:T(512)S(1)} %eq.754), kind=kOutput, calls=%fused_computation.3 | convolution fusion | flops 16323641344 | bytes 31852544 | tf_op jit(solution)/shard_map/bs,bx->sx/dot_general | solution.py:125
  300.4 19.8 %reshape.426 = f32[16,16,2,72,72]{4,3,2,1,0:T(8,128)} reshape(f32[256,10368]{1,0:T(8,128)} %fusion) | data formatting | bytes 21233664 | tf_op jit(solution)/shard_map/reshape | solution.py:126
  320.2 10.5 %copy.184 = f32[16,16,2,72,72]{4,1,3,0,2:T(8,128)S(1)} copy(f32[16,16,2,72,72]{4,3,2,1,0:T(8,128)} %reshape.426) | data formatting | bytes 21233664 | tf_op jit(solution)/shard_map/reshape | solution.py:126
  330.7 10.1 %slice.506 = f32[2,16,72,16,8]{4,3,2,1,0:T(8,128)} slice(f32[2,16,72,16,72]{4,3,2,1,0:T(8,128)S(1)} %bitcast.144), slice={[0:2], [0:16], [0:72], [0:16], [64:72]} | slice | bytes 2359296 | tf_op jit(solution)/shard_map/slice | solution.py:47
  340.8 2.0 copy-done.2
  342.8 16.6 %reshape.427 = f32[2,16,72,1024]{3,2,1,0:T(8,128)} reshape(f32[2,16,72,16,64]{4,3,2,1,0:T(8,128)} %bitcast.145) | data formatting | bytes 18874368 | tf_op jit(solution)/shard_map/reshape | solution.py:45
  359.4 12.9 %pad.33 = f32[2,16,72,16,64]{4,3,2,1,0:T(8,128)} pad(f32[2,16,72,16,8]{4,3,2,1,0:T(8,128)} %slice.506, f32[]{:T(128)} %constant.251.clone.1), padding=0_0x0_0x0_0x0_0x0_56 | pad | bytes 10616836 | tf_op jit(solution)/shard_map/jit(_pad)/pad | solution.py:47
  372.3 16.7 %reshape.428 = f32[2,16,72,1024]{3,2,1,0:T(8,128)} reshape(f32[2,16,72,16,64]{4,3,2,1,0:T(8,128)} %pad.33) | data formatting | bytes 18874368 | tf_op jit(solution)/shard_map/reshape | solution.py:48
  388.9 13.1 %add_bitcast_fusion = f32[2,1032,16,72]{1,3,2,0:T(8,128)} fusion(f32[2,16,72,1024]{3,2,1,0:T(8,128)} %reshape.428, f32[2,16,72,1024]{3,2,1,0:T(8,128)} %reshape.427), kind=kLoop, calls=%fused_computation.12 | loop fusion | flops 2377728 | bytes 28385280 | tf_op jit(solution)/shard_map/transpose | solution.py:128
  402.0 8.3 %slice.507 = f32[2,1032,16,64]{1,3,2,0:T(8,128)} slice(f32[2,1032,16,72]{1,3,2,0:T(8,128)} %add_bitcast_fusion), slice={[0:2], [0:1032], [0:16], [0:64]} | slice | bytes 16908288 | tf_op jit(solution)/shard_map/slice | solution.py:45
  410.3 9.4 %copy.171 = f32[2,1032,1024]{2,1,0:T(8,128)} copy(f32[2,1032,1024]{1,2,0:T(8,128)} %bitcast.148) | data formatting | bytes 16908288 | tf_op jit(solution)/shard_map/reshape | solution.py:45
  419.7 4.8 pad.36
  424.5 9.5 %copy.172 = f32[2,1032,1024]{2,1,0:T(8,128)} copy(f32[2,1032,1024]{1,2,0:T(8,128)} %bitcast.147) | data formatting | bytes 16908288 | tf_op jit(solution)/shard_map/reshape | solution.py:48
  434.0 12.1 %add_bitcast_fusion.1 = f32[2,1032,1032]{1,2,0:T(8,128)} fusion(f32[2,1032,1024]{2,1,0:T(8,128)} %copy.172, f32[2,1032,1024]{2,1,0:T(8,128)} %copy.171), kind=kLoop, calls=%fused_computation.13 | loop fusion | flops 2130048 | bytes 25428480 | tf_op jit(solution)/shard_map/transpose | solution.py:129
  446.1 1.3 slice.513
  447.8 3.6 collective-permute-start.1
  451.3 0.8 slice_bitcast_fusion
  452.2 1.3 collective-permute-start
  454.2 8.4 %slice.509 = f32[2,1024,1024]{1,2,0:T(8,128)} slice(f32[2,1032,1032]{1,2,0:T(8,128)} %add_bitcast_fusion.1), slice={[0:2], [0:1024], [0:1024]} | slice | bytes 16777216 | tf_op jit(solution)/shard_map/slice | solution.py:140
  462.5 5.2 %collective-permute-start.2 = (f32[2,8,8]{1,2,0:T(8,128)S(1)}, f32[2,8,8]{1,2,0:T(8,128)S(1)}, u32[]{:S(2)}, u32[]{:S(2)}) collective-permute-start(f32[2,8,8]{1,2,0:T(8,128)S(1)} %slice.515), channel_id=1, source_target_pairs={{0,36},{4,40},{8,44},{12,48},{16,52},{20,56},{24,60},{28,64},{32,6... | collective-permute-start | bytes 1544 | tf_op jit(solution)/shard_map/ppermute | solution.py:19
  468.1 1.5 fusion.207
  469.5 1.4 slice_add_fusion
  471.0 5.9 %scatter-add.11 = f32[1,1,2,1024,1024]{3,4,2,1,0:T(8,128)} dynamic-update-slice(f32[1,1,2,1024,1024]{3,4,2,1,0:T(8,128)} %bitcast.146, f32[1,1,2,8,1024]{3,4,2,1,0:T(8,128)S(1)} %bitcast.153, s32[]{:T(128)} %constant.247.clone.1, s32[]{:T(128)} %constant.247.clone.1, s32[]{:T(128)} %constant.247.clone.1, s32[]{:T(128)} %constant.247.clone.1, s32[]{:T(128)} %constant.247.clone.1) | dynamic-update-slice | bytes 131076 | tf_op jit(solution)/shard_map/scatter-add | solution.py:142
  476.9 2.6 scatter-add.14
  479.5 8.7 %copy.177 = f32[1,1,2,1024,1024]{4,3,2,1,0:T(8,128)} copy(f32[1,1,2,1024,1024]{3,4,2,1,0:T(8,128)} %scatter-add.14) | data formatting | bytes 16777216 | tf_op jit(solution)/shard_map/scatter-add | solution.py:143
  (89 shorter events, 12.1 us)
Async XLA Ops:
  0.0 91.4 %copy-start = (f32[16,8]{0,1:T(8,128)S(1)}, f32[16,8]{0,1:T(8,128)}, u32[]{:S(2)}) copy-start(f32[16,8]{0,1:T(8,128)} %param.19) | copy-start | bytes 1540
  4.5 21.9 %all-to-all-start = ((s32[64,4,2]{1,2,0:T(2,128)}), s32[64,4,2]{1,2,0:T(2,128)S(1)}, u32[]{:S(2)}, u32[]{:S(2)}) async-start(s32[64,4,2]{1,2,0:T(2,128)} %copy.151), calls=%async_computation | async-start | bytes 131072 | tf_op jit(solution)/shard_map/all_to_all | solution.py:94
  26.4 17.6 %all-to-all-start.2 = ((s32[64,4,2,1,128]{4,2,1,3,0:T(2,128)}), s32[64,4,2,1,128]{4,2,1,3,0:T(2,128)S(1)}, u32[]{:S(2)}, u32[]{:S(2)}) async-start(s32[64,4,2,1,128]{4,2,1,3,0:T(2,128)} %bitcast.4), calls=%async_computation.2 | async-start | bytes 524288 | tf_op jit(solution)/shard_map/all_to_all | solution.py:87
  44.0 8.6 %all-to-all-start.1 = ((s32[4,1,128]{2,1,0:T(1,128)}), s32[4,1,128]{2,1,0:T(1,128)S(1)}, u32[]{:S(2)}, u32[]{:S(2)}) async-start(s32[4,1,128]{2,1,0:T(1,128)} %reshape.471), calls=%async_computation.1 | async-start | bytes 4096 | tf_op jit(solution)/shard_map/all_to_all | solution.py:93
  52.6 32.6 %all-to-all-start.3 = ((s32[64,4,2,1,128]{4,2,0,3,1:T(2,128)}), s32[64,4,2,1,128]{4,2,0,3,1:T(2,128)S(1)}, u32[]{:S(2)}, u32[]{:S(2)}) async-start(s32[64,4,2,1,128]{4,2,0,3,1:T(2,128)} %copy.155), calls=%async_computation.3 | async-start | bytes 524288 | tf_op jit(solution)/shard_map/all_to_all | solution.py:86
  85.2 64.3 %all-to-all-start.4 = ((f32[64,4,2,2,128]{4,3,2,1,0:T(2,128)}), f32[64,4,2,2,128]{4,3,2,1,0:T(2,128)S(1)}, u32[]{:S(2)}, u32[]{:S(2)}) async-start(f32[64,4,2,2,128]{4,3,2,1,0:T(2,128)} %bitcast.15), calls=%async_computation.4 | async-start | bytes 1048576 | tf_op jit(solution)/shard_map/all_to_all | solution.py:80
  150.4 13.2 %all-to-all-start.5 = ((f32[64,4,2,2,128]{4,3,2,0,1:T(2,128)}), f32[64,4,2,2,128]{4,3,2,0,1:T(2,128)S(1)}, u32[]{:S(2)}, u32[]{:S(2)}) async-start(f32[64,4,2,2,128]{4,3,2,0,1:T(2,128)} %copy.157), calls=%async_computation.5 | async-start | bytes 1048576 | tf_op jit(solution)/shard_map/all_to_all | solution.py:79
  182.1 8.5 %copy-start.19 = (s32[128,128]{1,0:T(8,128)S(1)}, s32[128,128]{1,0:T(8,128)}, u32[]{:S(2)}) copy-start(s32[128,128]{1,0:T(8,128)} %get-tuple-element.143) | copy-start | bytes 196612
  208.0 8.6 %copy-start.9 = (f32[128,128,1]{1,2,0:T(1,128)S(1)}, f32[128,128,1]{1,2,0:T(1,128)}, u32[]{:S(2)}) copy-start(f32[128,128,1]{1,2,0:T(1,128)} %get-tuple-element.105) | copy-start | bytes 196612
  208.0 8.6 %copy-start.10 = (f32[128,128,1]{1,2,0:T(1,128)S(1)}, f32[128,128,1]{1,2,0:T(1,128)}, u32[]{:S(2)}) copy-start(f32[128,128,1]{1,2,0:T(1,128)} %get-tuple-element.106) | copy-start | bytes 196612
  208.0 8.6 %copy-start.11 = (f32[128,128,1]{1,2,0:T(1,128)S(1)}, f32[128,128,1]{1,2,0:T(1,128)}, u32[]{:S(2)}) copy-start(f32[128,128,1]{1,2,0:T(1,128)} %get-tuple-element.107) | copy-start | bytes 196612
  208.0 8.6 %copy-start.12 = (f32[128,128,1]{1,2,0:T(1,128)S(1)}, f32[128,128,1]{1,2,0:T(1,128)}, u32[]{:S(2)}) copy-start(f32[128,128,1]{1,2,0:T(1,128)} %get-tuple-element.108) | copy-start | bytes 196612
  208.0 8.6 %copy-start.13 = (f32[128,128,1]{1,2,0:T(1,128)S(1)}, f32[128,128,1]{1,2,0:T(1,128)}, u32[]{:S(2)}) copy-start(f32[128,128,1]{1,2,0:T(1,128)} %get-tuple-element.109) | copy-start | bytes 196612
  208.0 8.6 %copy-start.14 = (f32[128,128,1]{1,2,0:T(1,128)S(1)}, f32[128,128,1]{1,2,0:T(1,128)}, u32[]{:S(2)}) copy-start(f32[128,128,1]{1,2,0:T(1,128)} %get-tuple-element.110) | copy-start | bytes 196612
  208.0 8.6 %copy-start.15 = (f32[128,128,1]{1,2,0:T(1,128)S(1)}, f32[128,128,1]{1,2,0:T(1,128)}, u32[]{:S(2)}) copy-start(f32[128,128,1]{1,2,0:T(1,128)} %get-tuple-element.111) | copy-start | bytes 196612
  208.0 8.6 %copy-start.16 = (f32[128,128,1]{1,2,0:T(1,128)S(1)}, f32[128,128,1]{1,2,0:T(1,128)}, u32[]{:S(2)}) copy-start(f32[128,128,1]{1,2,0:T(1,128)} %get-tuple-element.112) | copy-start | bytes 196612
  208.0 8.6 %copy-start.18 = (s32[128,128]{1,0:T(8,128)S(1)}, s32[128,128]{1,0:T(8,128)}, u32[]{:S(2)}) copy-start(s32[128,128]{1,0:T(8,128)} %get-tuple-element.137) | copy-start | bytes 196612
  234.1 8.5 %copy-start.3 = (s32[128,128]{1,0:T(8,128)S(1)}, s32[128,128]{1,0:T(8,128)}, u32[]{:S(2)}) copy-start(s32[128,128]{1,0:T(8,128)} %get-tuple-element.160) | copy-start | bytes 196612
  234.1 8.5 %copy-start.4 = (s32[128,128]{1,0:T(8,128)S(1)}, s32[128,128]{1,0:T(8,128)}, u32[]{:S(2)}) copy-start(s32[128,128]{1,0:T(8,128)} %get-tuple-element.161) | copy-start | bytes 196612
  234.1 8.5 %copy-start.5 = (s32[128,128]{1,0:T(8,128)S(1)}, s32[128,128]{1,0:T(8,128)}, u32[]{:S(2)}) copy-start(s32[128,128]{1,0:T(8,128)} %get-tuple-element.162) | copy-start | bytes 196612
  234.1 8.5 %copy-start.6 = (s32[128,128]{1,0:T(8,128)S(1)}, s32[128,128]{1,0:T(8,128)}, u32[]{:S(2)}) copy-start(s32[128,128]{1,0:T(8,128)} %get-tuple-element.163) | copy-start | bytes 196612
  234.2 8.5 %copy-start.7 = (s32[128,128]{1,0:T(8,128)S(1)}, s32[128,128]{1,0:T(8,128)}, u32[]{:S(2)}) copy-start(s32[128,128]{1,0:T(8,128)} %get-tuple-element.164) | copy-start | bytes 196612
  234.2 8.5 %copy-start.8 = (s32[128,128]{1,0:T(8,128)S(1)}, s32[128,128]{1,0:T(8,128)}, u32[]{:S(2)}) copy-start(s32[128,128]{1,0:T(8,128)} %get-tuple-element.165) | copy-start | bytes 196612
  234.2 8.5 %copy-start.17 = (s32[128,128]{1,0:T(8,128)S(1)}, s32[128,128]{1,0:T(8,128)}, u32[]{:S(2)}) copy-start(s32[128,128]{1,0:T(8,128)} %get-tuple-element.41) | copy-start | bytes 196612
  330.7 12.1 %copy-start.2 = (f32[16,16,2,72,72]{4,1,3,0,2:T(8,128)}, f32[16,16,2,72,72]{4,1,3,0,2:T(8,128)S(1)}, u32[]{:S(2)}) copy-start(f32[16,16,2,72,72]{4,1,3,0,2:T(8,128)S(1)} %copy.184) | copy-start | bytes 31850500
  410.3 9.4 %slice-start = ((f32[2,1032,16,72]{1,3,2,0:T(8,128)}), f32[2,1032,16,8]{1,3,2,0:T(8,128)S(1)}, s32[]{:S(2)}) async-start(f32[2,1032,16,72]{1,3,2,0:T(8,128)} %add_bitcast_fusion), calls=%async_computation.6 | async-start | bytes 2359296 | tf_op jit(solution)/shard_map/slice | solution.py:47
  447.8 19.9 %collective-permute-start.1 = (f32[2,8,1024]{2,1,0:T(8,128)S(1)}, f32[2,8,1024]{2,1,0:T(8,128)S(1)}, u32[]{:S(2)}, u32[]{:S(2)}) collective-permute-start(f32[2,8,1024]{2,1,0:T(8,128)S(1)} %copy.173), channel_id=1, source_target_pairs={{0,32},{4,36},{8,40},{12,44},{16,48},{20,52},{24,56},{28,60},{32,6... | collective-permute-start | bytes 196616 | tf_op jit(solution)/shard_map/ppermute | solution.py:19
  452.2 15.9 %collective-permute-start = (f32[2,8,1024]{2,1,0:T(8,128)S(1)}, f32[2,8,1024]{2,1,0:T(8,128)S(1)}, u32[]{:S(2)}, u32[]{:S(2)}) collective-permute-start(f32[2,8,1024]{2,1,0:T(8,128)S(1)} %slice_bitcast_fusion), channel_id=1, source_target_pairs={{0,4},{4,8},{8,12},{12,16},{16,20},{20,24},{24,28},{28,32},{32,36}... | collective-permute-start | bytes 196616 | tf_op jit(solution)/shard_map/ppermute | solution.py:19
  462.5 14.3 %collective-permute-start.2 = (f32[2,8,8]{1,2,0:T(8,128)S(1)}, f32[2,8,8]{1,2,0:T(8,128)S(1)}, u32[]{:S(2)}, u32[]{:S(2)}) collective-permute-start(f32[2,8,8]{1,2,0:T(8,128)S(1)} %slice.515), channel_id=1, source_target_pairs={{0,36},{4,40},{8,44},{12,48},{16,52},{20,56},{24,60},{28,64},{32,6... | collective-permute-start | bytes 1544 | tf_op jit(solution)/shard_map/ppermute | solution.py:19
  476.9 11.3 %copy-start.1 = (f32[16,8]{0,1:T(8,128)S(1)}, f32[16,8]{0,1:T(8,128)}, u32[]{:S(2)}) copy-start(f32[16,8]{0,1:T(8,128)} %param.19) | copy-start | bytes 1540
where the time goes:
time: 498 us; the launch traced here: 488 us
  local copies, waits for them, and re-layouts  220 us (44%)
  matrix products  108 us (22%)
  other arithmetic  84 us (17%)
  starting transfers between devices  46.4 us (9%)
  waiting for transfers between devices  29.3 us (6%)
    dot_general x4, matrix products, shards(): jnp.einsum('bcru,brv->bcuv', weighted, rows_along_v, precision=highest)  70.1 us
    add x4, other arithmetic, spread_matrix(): matrix + jnp.where(places == first_cell[..., None] + tap_index, taps[...,...  47.3 us
    dot_general x4, local copies, waits for them, and re-layouts, shards(): jnp.einsum('bcru,brv->bcuv', weighted, rows_along_v, precision=highest)  33.9 us
    dot_general x1, matrix products, shards(): accum = jnp.einsum('bs,bx->sx', chosen, all_patches, precision=highest)  31.7 us
    reshape x2, local copies, waits for them, and re-layouts, shards(): accum.reshape(patches_across, patches_across, 2, extent, extent)  30.3 us
    reshape x2, local copies, waits for them, and re-layouts, unfold_edges(): edge_part = edge_part.reshape(leading + (block_count * SUB,))  26.2 us
    reshape x2, local copies, waits for them, and re-layouts, unfold_edges(): core_part = patches[..., :SUB].reshape(leading + (block_count * SUB,))  26 us
    scatter x2, local copies, waits for them, and re-layouts, bucket(): buffer = buffer.at[slot_index].set(values)  25.6 us
  transfers between devices with their start and end apart: 9, of which 4 were waited for; matrix products, arithmetic and copies ran while one was open for 23% of the time, Pallas kernels for 0%

commit v1 on v0

v1 whole, which is shorter than its diff:
```python
import functools

import jax
import jax.numpy as jnp
from jax import lax
from jax.experimental import pallas as pl
from jax.experimental.pallas import tpu as pltpu
from jax.sharding import PartitionSpec as P

TCOLS = 8
SUB = 64
KW = 8
OVER = 16
TILE = 1024
SIDE = TILE // SUB
PATCHES = SIDE * SIDE
EXT = SUB + KW
BLOCKS = 256
ZS, XS, YS, CORES = 8, 4, 4, 2
FAR = [(dz, dc) for dz in (4, 3, 5, 2, 6, 1, 7, 0) for dc in (0, 1)]
FAR = [step for step in FAR if step != (0, 0)] + [(0, 0)]
NEAR = [(dx, dy) for dx in (2, 1, 3, 0) for dy in (2, 1, 3, 0)]
GROUP = 16
HALVES = 2
MESH = pl.DeviceIdType.MESH
bf16, f32, i32 = jnp.bfloat16, jnp.float32, jnp.int32


def position():
    tile, y = lax.axis_index("tile"), lax.axis_index("wp")
    return tile // (XS * CORES), (tile // CORES) % XS, tile % CORES, y


def exchange_kernel(source_ref, patch_ref, vis_ref, weight_ref, cell_ref, tap_ref, got_ref,
                    outgoing, middle, far_out, far_in, near_out, near_in, local):
    z, x, core, y = position()

    def far_device(step, sign=1):
        dz, dc = step
        return ((((z + sign * dz + ZS) % ZS) * XS + x) * CORES + (core + dc) % CORES, y)

    def near_device(step, sign=1):
        dx, dy = step
        return ((z * XS + (x + sign * dx + XS) % XS) * CORES + core, (y + sign * dy + YS) % YS)

    barrier = pltpu.get_barrier_semaphore()
    for step in FAR[:-1]:
        pl.semaphore_signal(barrier, inc=1, device_id=far_device(step), device_id_type=MESH)
    for step in NEAR[:-1]:
        pl.semaphore_signal(barrier, inc=1, device_id=near_device(step), device_id_type=MESH)

    lane = lax.broadcasted_iota(i32, (1, 128), 1)

    def fill(far_index):
        dz, dc = FAR[far_index]
        to_z, to_core = (z + dz) % ZS, (core + dc) % CORES

        def one(near_index, carry):
            group = near_index // YS
            dx = jnp.where(group == 0, 2, jnp.where(group == 1, 1, jnp.where(group == 2, 3, 0)))
            group = near_index % YS
            dy = jnp.where(group == 0, 2, jnp.where(group == 1, 1, jnp.where(group == 2, 3, 0)))
            target = ((to_z * XS + (x + dx) % XS) * CORES + to_core) * YS + (y + dy) % YS
            spot = 2 * (near_index * GROUP + far_index) % 128
            patches = jnp.zeros((1, 128), i32)
            for slot in range(2):
                block = source_ref[slot, target]
                valid = jnp.where(block < BLOCKS, 1.0, 0.0).astype(f32)
                block = jnp.minimum(block, BLOCKS - 1)
                weight = weight_ref[pl.ds(block, 1), :] * valid
                outgoing[far_index, near_index, 3 * slot:3 * slot + 2, :] = vis_ref[block] * weight
                code = cell_ref[pl.ds(block, 1), :] * (OVER * OVER) + tap_ref[pl.ds(block, 1), :]
                outgoing[far_index, near_index, 3 * slot + 2:3 * slot + 3, :] = code.astype(f32)
                patches = jnp.where(lane == spot + slot, patch_ref[block], patches)
            outgoing[far_index, near_index, 6:7, :] = patches.astype(f32)
            outgoing[far_index, near_index, 7:8, :] = jnp.zeros((1, 128), f32)
            return carry

        lax.fori_loop(0, GROUP, one, 0, unroll=4)

    copies = []
    for index, step in enumerate(FAR):
        fill(index)
        if index == 0:
            pl.semaphore_wait(barrier, len(FAR) + len(NEAR) - 2)
        if index < GROUP - 1:
            copy = pltpu.make_async_remote_copy(
                src_ref=outgoing.at[index], dst_ref=middle.at[index],
                send_sem=far_out.at[index], recv_sem=far_in.at[index],
                device_id=far_device(step), device_id_type=MESH)
        else:
            copy = pltpu.make_async_copy(outgoing.at[index], middle.at[index], local.at[0])
        copy.start()
        copies.append(copy)

    part = GROUP // HALVES
    sends = []
    for half in range(HALVES):
        rows = pl.ds(half * part, part)
        for index in range(half * part, (half + 1) * part):
            if index < GROUP - 1:
                copies[index].wait_recv()
            else:
                copies[index].wait()
        for index, step in enumerate(NEAR):
            number = half * GROUP + index
            if index < GROUP - 1:
                copy = pltpu.make_async_remote_copy(
                    src_ref=middle.at[rows, index], dst_ref=got_ref.at[index, rows],
                    send_sem=near_out.at[number], recv_sem=near_in.at[number],
                    device_id=near_device(step), device_id_type=MESH)
            else:
                copy = pltpu.make_async_copy(
                    middle.at[rows, index], got_ref.at[index, rows], local.at[1 + half])
            copy.start()
            sends.append(copy)
    for copy in sends:
        copy.wait()
    for copy in copies[:-1]:
        copy.wait_send()


def exchange(source, patch_index, visibilities, vis_weight, cell_index, tap_offsets):
    vmem, smem = pl.BlockSpec(memory_space=pltpu.VMEM), pl.BlockSpec(memory_space=pltpu.SMEM)
    shape = (GROUP, GROUP, 8, 128)
    return pl.pallas_call(
        exchange_kernel,
        out_shape=jax.ShapeDtypeStruct(shape, f32),
        in_specs=[smem, smem] + [vmem] * 4,
        out_specs=vmem,
        scratch_shapes=[
            pltpu.VMEM(shape, f32), pltpu.VMEM(shape, f32),
            pltpu.SemaphoreType.DMA((GROUP,)), pltpu.SemaphoreType.DMA((GROUP,)),
            pltpu.SemaphoreType.DMA((HALVES * GROUP,)), pltpu.SemaphoreType.DMA((HALVES * GROUP,)),
            pltpu.SemaphoreType.DMA((1 + HALVES,)),
        ],
        compiler_params=pltpu.CompilerParams(
            collective_id=0, has_side_effects=True, vmem_limit_bytes=32 << 20),
    )(source, patch_index, visibilities, vis_weight, cell_index, tap_offsets)


UNROLL = 16
ROWS = 2 * EXT


def place(cell, row):
    step = (cell - row + 15) >> 4
    inside = (step * 16 + row - cell) < KW
    return jnp.where(inside, step, 99).astype(jnp.int16)


def halves(value):
    high = value.astype(bf16).astype(f32)
    rest = value - high
    return (jnp.concatenate([high, high], 0).astype(bf16), jnp.concatenate([rest, rest], 0).astype(bf16))


def contract(left, right):
    return lax.dot_general(left, right, (((1,), (1,)), ((), ())), preferred_element_type=f32)


def grid_kernel(got_ref, table_ref, tile_ref, right_ref, lower_ref, corner_ref,
                total, patch_rows, patch_smem, stage, patch_sem, stage_sem):
    for quarter in range(4):
        rows = jnp.sum(got_ref[pl.ds(quarter * 64, 64), 6, :], axis=0, keepdims=True)
        patch_rows[quarter:quarter + 1, :] = rows.astype(i32)
    numbers = pltpu.make_async_copy(patch_rows, patch_smem, patch_sem)
    numbers.start()

    def clear(k, carry):
        total[pl.ds(k * 4, 4)] = jnp.zeros((4, ROWS, 128), f32)
        return carry

    lax.fori_loop(0, (PATCHES + SIDE) // 4, clear, 0)
    numbers.wait()

    row8 = lax.broadcasted_iota(i32, (8, 128), 0)
    row16 = lax.broadcasted_iota(i32, (16, 128), 0)
    table = table_ref[...]
    zero = jnp.zeros((16, 128), bf16)

    def spread(masks, value):
        return jnp.concatenate([jnp.where(mask, value, zero) for mask in masks], 0)

    def one(pair, slot):
        real = got_ref[pair, pl.ds(3 * slot, 1), :]
        imag = got_ref[pair, pl.ds(3 * slot + 1, 1), :]
        code = jnp.broadcast_to(got_ref[pair, pl.ds(3 * slot + 2, 1), :], (8, 128)).astype(i32)
        cell_u = code >> 14
        cell_v = (code >> 8) & (SUB - 1)
        ku = jnp.take_along_axis(table, ((code >> 1) & 0x78) + ((row8 - cell_u) & 7), axis=1)
        kv = jnp.take_along_axis(table, ((code << 3) & 0x78) + ((row8 - cell_v) & 7), axis=1)
        step_u = place(jnp.concatenate([cell_u, cell_u], 0), row16)
        step_v = place(jnp.concatenate([cell_v, cell_v], 0), row16)
        masks_u = [step_u == jnp.int16(t) for t in range(5)]
        masks_v = [step_v == jnp.int16(t) for t in range(5)]
        v_high, v_rest = halves(kv)
        r_high, r_rest = halves(ku * real)
        i_high, i_rest = halves(ku * imag)
        v_high, v_rest = spread(masks_v, v_high), spread(masks_v, v_rest)
        u_high = jnp.concatenate([spread(masks_u, r_high), spread(masks_u, i_high)], 0)
        u_rest = jnp.concatenate([spread(masks_u, r_rest), spread(masks_u, i_rest)], 0)
        out = contract(jnp.concatenate([u_high, u_rest], 1), jnp.concatenate([v_high, v_high], 1))
        out = out + contract(u_high, v_rest)
        number = 2 * pair + slot
        patch = patch_smem[number // 128, number % 128] + SIDE
        total[patch, 0:EXT, 0:80] = total[patch, 0:EXT, 0:80] + out[0:EXT]
        total[patch, EXT:ROWS, 0:80] = total[patch, EXT:ROWS, 0:80] + out[80:80 + EXT]

    def several(k, carry):
        for q in range(UNROLL):
            for slot in range(2):
                one(k * UNROLL + q, slot)
        return carry

    lax.fori_loop(0, BLOCKS // UNROLL, several, 0)

    lane = lax.broadcasted_iota(i32, (8, 128), 1)
    right_ref[...] = jnp.zeros_like(right_ref)

    def joined(load, put):
        before = jnp.zeros((8, 128), f32)
        for pair in range(SIDE // 2):
            moved = pltpu.roll(load(2 * pair + 1), SUB, 1)
            put(pair, load(2 * pair) + jnp.where(lane >= SUB, moved, before))
            before = moved
        return jnp.where(lane < KW, before, 0.0)

    def stripe(patch_row, slot):
        for part in range(2):
            for step in range(SUB // 8):
                start = part * EXT + step * 8

                def load(column):
                    value = total[(patch_row + 1) * SIDE + column, start:start + 8, :]
                    if step == 0:
                        last = part * EXT + SUB
                        value = value + total[patch_row * SIDE + column, last:last + 8, :]
                    return value

                def put(pair, value):
                    stage[slot, part, step * 8:step * 8 + 8, pair * 128:pair * 128 + 128] = value

                past = joined(load, put)
                rows = slice(step * 8, step * 8 + 8)
                right_ref[part, rows, :] = right_ref[part, rows, :] + pltpu.roll(past, patch_row * KW, 1)

    def write(patch_row, slot):
        return pltpu.make_async_copy(
            stage.at[slot], tile_ref.at[:, pl.ds(patch_row * SUB, SUB), :], stage_sem.at[slot])

    def two(k, carry):
        for slot in range(2):
            @pl.when(k > 0)
            def _():
                write(2 * k - 2 + slot, slot).wait()
            stripe(2 * k + slot, slot)
            write(2 * k + slot, slot).start()
        return carry

    lax.fori_loop(0, SIDE // 2, two, 0)

    for part in range(2):
        last = part * EXT + SUB

        def load(column):
            return total[SIDE * SIDE + column, last:last + 8, :]

        def put(pair, value):
            lower_ref[part, :, pair * 128:pair * 128 + 128] = value

        corner_ref[part] = joined(load, put)
    for slot in range(2):
        write(SIDE - 2 + slot, slot).wait()


def make_tile(got, table):
    vmem = pl.BlockSpec(memory_space=pltpu.VMEM)
    return pl.pallas_call(
        grid_kernel,
        out_shape=(
            jax.ShapeDtypeStruct((2, TILE, TILE), f32), jax.ShapeDtypeStruct((2, SUB, 128), f32),
            jax.ShapeDtypeStruct((2, KW, TILE), f32), jax.ShapeDtypeStruct((2, KW, 128), f32)),
        in_specs=[vmem, vmem],
        out_specs=(pl.BlockSpec(memory_space=pl.ANY), vmem, vmem, vmem),
        scratch_shapes=[
            pltpu.VMEM((PATCHES + SIDE, ROWS, 128), f32),
            pltpu.VMEM((4, 128), i32), pltpu.SMEM((4, 128), i32),
            pltpu.VMEM((2, 2, SUB, TILE), f32),
            pltpu.SemaphoreType.DMA, pltpu.SemaphoreType.DMA((2,)),
        ],
        compiler_params=pltpu.CompilerParams(vmem_limit_bytes=48 << 20),
    )(got, table)


def margins_kernel(right_ref, lower_ref, corner_ref, left_in, upper_in, corner_in, out_sem, in_sem):
    tile, y = lax.axis_index("tile"), lax.axis_index("wp")
    tiles = ZS * XS * CORES
    barrier = pltpu.get_barrier_semaphore()
    steps = (1, TCOLS, TCOLS + 1)
    for step in steps:
        for to in ((tile + step) % tiles, (tile + tiles - step) % tiles):
            pl.semaphore_signal(barrier, inc=1, device_id=(to, y), device_id_type=MESH)
    pl.semaphore_wait(barrier, 2 * len(steps))
    copies = []
    for index, (source, target) in enumerate(
            ((right_ref, left_in), (lower_ref, upper_in), (corner_ref, corner_in))):
        copy = pltpu.make_async_remote_copy(
            src_ref=source, dst_ref=target, send_sem=out_sem.at[index], recv_sem=in_sem.at[index],
            device_id=((tile + steps[index]) % tiles, y), device_id_type=MESH)
        copy.start()
        copies.append(copy)
    for copy in copies:
        copy.wait()


def margins(right, lower, corner):
    vmem = pl.BlockSpec(memory_space=pltpu.VMEM)
    return pl.pallas_call(
        margins_kernel,
        out_shape=tuple(jax.ShapeDtypeStruct(a.shape, a.dtype) for a in (right, lower, corner)),
        in_specs=[vmem] * 3,
        out_specs=(vmem,) * 3,
        scratch_shapes=[pltpu.SemaphoreType.DMA((3,)), pltpu.SemaphoreType.DMA((3,))],
        compiler_params=pltpu.CompilerParams(collective_id=1, has_side_effects=True),
    )(right, lower, corner)


def finish_kernel(tile_in, left_in, upper_in, corner_in, tile_ref, side, top, sems):
    del tile_in
    tile = lax.axis_index("tile")
    has_left = jnp.where(tile % TCOLS > 0, 1.0, 0.0).astype(f32)
    has_upper = jnp.where(tile // TCOLS > 0, 1.0, 0.0).astype(f32)
    sides = tile_ref.at[:, :, pl.ds(0, 128)]
    tops = tile_ref.at[:, pl.ds(0, KW), pl.ds(128, TILE - 128)]
    read_side = pltpu.make_async_copy(sides, side, sems.at[0])
    read_top = pltpu.make_async_copy(tops, top, sems.at[1])
    read_side.start()
    read_top.start()
    lane = lax.broadcasted_iota(i32, (SUB, 128), 1)
    read_top.wait()
    top[...] = top[...] + upper_in[:, :, 128:] * has_upper
    write_top = pltpu.make_async_copy(top, tops, sems.at[1])
    write_top.start()
    read_side.wait()
    for part in range(2):
        packed = left_in[part] * has_left
        for patch_row in range(SIDE):
            rows = slice(patch_row * SUB, patch_row * SUB + SUB)
            moved = packed if patch_row == 0 else pltpu.roll(packed, 128 - KW * patch_row, 1)
            side[part, rows, :] = side[part, rows, :] + jnp.where(lane < KW, moved, 0.0)
        side[part, 0:KW, :] = (side[part, 0:KW, :] + upper_in[part, :, 0:128] * has_upper
                               + corner_in[part] * (has_left * has_upper))
    write_side = pltpu.make_async_copy(side, sides, sems.at[0])
    write_side.start()
    write_top.wait()
    write_side.wait()


def finish(tile, left, upper, corner):
    vmem, hbm = pl.BlockSpec(memory_space=pltpu.VMEM), pl.BlockSpec(memory_space=pl.ANY)
    return pl.pallas_call(
        finish_kernel,
        out_shape=jax.ShapeDtypeStruct(tile.shape, tile.dtype),
        in_specs=[hbm, vmem, vmem, vmem],
        out_specs=hbm,
        scratch_shapes=[
            pltpu.VMEM((2, TILE, 128), f32), pltpu.VMEM((2, KW, TILE - 128), f32),
            pltpu.SemaphoreType.DMA((2,))],
        input_output_aliases={0: 0},
        compiler_params=pltpu.CompilerParams(vmem_limit_bytes=16 << 20),
    )(tile, left, upper, corner)


def shards(visibilities, vis_weight, cell_index, tap_offsets, routes, patch_index, kernel):
    blocks = visibilities.shape[0]
    block_ids = lax.broadcasted_iota(i32, (blocks, blocks), 0)
    named = routes == lax.broadcasted_iota(i32, (blocks, blocks), 1)
    first = jnp.min(jnp.where(named, block_ids, blocks), axis=0)
    last = jnp.max(jnp.where(named, block_ids, -1), axis=0)
    source = jnp.stack([first, jnp.where(last > first, last, blocks)])
    got = exchange(source, patch_index, visibilities, vis_weight, cell_index, tap_offsets)
    table = jnp.broadcast_to(kernel.reshape(1, OVER * KW), (8, OVER * KW))
    tile, right, lower, corner = make_tile(got.reshape(BLOCKS, 8, 128), table)
    tile = finish(tile, *margins(right, lower, corner))
    return tile.reshape(1, 1, 2, TILE, TILE)


def solution(mesh):
    in_specs = (
        P(("tile", "wp"), None, None),
        P(("tile", "wp"), None),
        P(("tile", "wp"), None),
        P(("tile", "wp"), None),
        P(("tile", "wp"), None),
        P(("tile", "wp")),
        P(),
    )
    out_specs = P("wp", "tile", None, None, None)
    return jax.shard_map(shards, mesh=mesh, in_specs=in_specs, out_specs=out_specs, check_vma=False)
```

time: 498 us -> 102 us (0.20); the launches traced: 488 us -> 101 us
  local copies, waits for them, and re-layouts: 220 us -> 9.4 us
  matrix products: 108 us -> 0 us
  Pallas kernels: 0 us -> 90.6 us
  other arithmetic: 84 us -> 0.83 us
  starting transfers between devices: 46.4 us -> 0 us
  waiting for transfers between devices: 29.3 us -> 0 us
    dot_general x13 -> x0, matrix products: 108 us -> none  [the longest x4 70.1 us: shards(): jnp.einsum('bcru,brv->bcuv', weighted, rows_along_v, precision=highest)]
    pallas_call x0 -> x4, Pallas kernels: none -> 90.6 us  [the longest x1 44.6 us: exchange(): pl.pallas_call(exchange_kernel, out_shape=jax.ShapeDtypeStruct(shape, f32...]
    reshape x8 -> x0, local copies, waits for them, and re-layouts: 83.7 us -> none  [the longest x2 30.3 us: shards(): accum.reshape(patches_across, patches_across, 2, extent, extent)]
    add x13 -> x0, other arithmetic: 51.2 us -> none  [the longest x4 47.3 us: spread_matrix(): matrix + jnp.where(places == first_cell[..., None] + tap_index, taps[...,...]
    all_to_all x6 -> x0, starting transfers between devices: 36.4 us -> none  [the longest x1 11.9 us: shards(): lax.all_to_all(sent_patch, 'tile', split_axis=0, concat_axis=0, tiled=True)]
    dot_general x4 -> x0, local copies, waits for them, and re-layouts: 33.9 us -> none  [shards(): jnp.einsum('bcru,brv->bcuv', weighted, rows_along_v, precision=highest)]
    slice x21 -> x0, local copies, waits for them, and re-layouts: 33.9 us -> none  [the longest x3 10.1 us: unfold_edges(): patches[..., SUB:]]
    all_to_all x6 -> x0, waiting for transfers between devices: 29.3 us -> none  [the longest x1 12.2 us: shards(): lax.all_to_all(sent_ints, 'tile', split_axis=0, concat_axis=0, tiled=True)]
  transfers between devices with their start and end apart: 9 -> 0, of which waited for: 4 -> 0; matrix products, arithmetic and copies ran while one was open for 23% -> 0% of each run, Pallas kernels for 0% -> 0%
where the time goes in v1:
time: 102 us; the launch traced here: 101 us
  Pallas kernels  90.6 us (89%)
  local copies, waits for them, and re-layouts  9.4 us (9%)
    pallas_call x1, Pallas kernels, exchange(): pl.pallas_call(exchange_kernel, out_shape=jax.ShapeDtypeStruct(shape, f32...  44.6 us
    pallas_call x1, Pallas kernels, make_tile(): pl.pallas_call(grid_kernel, out_shape=(jax.ShapeDtypeStruct((2, TILE, TIL...  31.8 us
    pallas_call x1, Pallas kernels, margins(): pl.pallas_call(margins_kernel, out_shape=tuple((jax.ShapeDtypeStruct(a.sh...  11.6 us
    unnamed x23, local copies, waits for them, and re-layouts  9.31 us
    pallas_call x1, Pallas kernels, finish(): pl.pallas_call(finish_kernel, out_shape=jax.ShapeDtypeStruct(tile.shape,...  2.53 us

profile of v1, /device:TPU:8, one launch (start us, length us, event | category | flops | bytes accessed | tf_op | source)
XLA Modules:
  0.0 100.9 jit_solution(8051917413658666975)
XLA Ops:
  0.0 0.8 select_reduce_fusion.1
  0.8 0.8 copy.11
  1.6 0.1 broadcast_in_dim.21
  1.7 0.0 copy-start
  1.7 0.9 copy-done
  2.7 0.0 copy-start.1
  2.7 0.9 copy-done.1
  3.6 0.0 copy-start.2
  3.6 0.9 copy-done.2
  4.5 0.0 copy-start.3
  4.5 0.9 copy-done.3
  5.4 0.0 copy-start.10
  5.4 0.7 copy-done.10
  6.1 44.6 %shard_map.73 = f32[16,16,8,128]{3,2,1,0:T(8,128)S(1)} custom-call(s32[2,256]{1,0:T(2,128)S(1)} %pad_add_fusion.source_ref, s32[256]{0:T(256)S(1)} %copy-done.10, f32[256,2,128]{2,1,0:T(2,128)S(1)} %copy-done, f32[256,128]{1,0:T(8,128)S(1)} %copy-done.1, s32[256,128]{1,0:T(8,128)S(1)} %copy-done.2, s32[256,128]{1,0:T(8,128)S(1)} %copy-done.3), custom_call_target="tpu_custom_call" | custom-call | tf_op jit(solution)/shard_map/pallas_call | solution.py:126
  50.7 31.8 %shard_map.74 = (f32[2,1024,1024]{2,1,0:T(8,128)}, f32[2,64,128]{2,1,0:T(8,128)S(1)}, f32[2,8,1024]{2,1,0:T(8,128)S(1)}, f32[2,8,128]{2,1,0:T(8,128)S(1)}) custom-call(f32[256,8,128]{2,1,0:T(8,128)S(1)} %bitcast.5, f32[8,128]{1,0:T(8,128)S(1)} %broadcast_in_dim.22.table_ref), custom_call_target="tpu_custom_call" | custom-call | tf_op jit(solution)/shard_map/pallas_call | solution.py:279
  82.5 0.0 copy-start.6
  82.6 0.6 copy-done.6
  83.2 0.0 copy-start.7
  83.2 0.6 copy-done.7
  83.8 0.0 copy-start.9
  83.8 0.6 copy-done.9
  84.4 11.6 %shard_map.75 = (f32[2,64,128]{2,1,0:T(8,128)}, f32[2,8,1024]{2,1,0:T(8,128)}, f32[2,8,128]{2,1,0:T(8,128)}) custom-call(f32[2,64,128]{2,1,0:T(8,128)} %copy-done.6, f32[2,8,1024]{2,1,0:T(8,128)} %copy-done.7, f32[2,8,128]{2,1,0:T(8,128)} %copy-done.9), custom_call_target="tpu_custom_call" | custom-call | tf_op jit(solution)/shard_map/pallas_call | solution.py:319
  96.0 0.0 copy-start.4
  96.0 0.8 copy-done.4
  96.8 0.0 copy-start.5
  96.8 0.8 copy-done.5
  97.7 0.0 copy-start.8
  97.7 0.7 copy-done.8
  98.4 2.5 %shard_map.76 = f32[2,1024,1024]{2,1,0:T(8,128)} custom-call(f32[2,1024,1024]{2,1,0:T(8,128)} %get-tuple-element.12.tile_in, f32[2,64,128]{2,1,0:T(8,128)S(1)} %copy-done.4, f32[2,8,1024]{2,1,0:T(8,128)S(1)} %copy-done.5, f32[2,8,128]{2,1,0:T(8,128)S(1)} %copy-done.8), custom_call_target="tpu_custom_call", output_to_operand_aliasing={{}: (0, {})} | custom-call | tf_op jit(solution)/shard_map/pallas_call | solution.py:362
  (3 shorter events, 0.0 us)
Async XLA Ops:
  1.7 1.0 copy-start
  2.7 0.9 copy-start.1
  3.6 0.9 copy-start.2
  4.5 0.9 copy-start.3
  5.4 0.7 copy-start.10
  82.5 0.6 copy-start.6
  83.2 0.6 copy-start.7
  83.8 0.6 copy-start.9
  96.0 0.8 copy-start.4
  96.8 0.8 copy-start.5
  97.7 0.7 copy-start.8

commit v2 on v1

v2 whole, which is shorter than its diff:
```python
import functools

import jax
import jax.numpy as jnp
from jax import lax
from jax.experimental import pallas as pl
from jax.experimental.pallas import tpu as pltpu
from jax.sharding import PartitionSpec as P

TCOLS = 8
SUB = 64
KW = 8
OVER = 16
TILE = 1024
SIDE = TILE // SUB
PATCHES = SIDE * SIDE
EXT = SUB + KW
BLOCKS = 256
ZS, XS, YS, CORES = 8, 4, 4, 2
GROUP = 16
LINES = 3 * GROUP + 2
EARLY = 8
MESH = pl.DeviceIdType.MESH
bf16, f32, i32 = jnp.bfloat16, jnp.float32, jnp.int32


def position():
    tile, y = lax.axis_index("tile"), lax.axis_index("wp")
    return tile // (XS * CORES), (tile // CORES) % XS, tile % CORES, y


def offset(order, size):
    if isinstance(order, int):
        return size // 2 + (order // 2 if order % 2 == 0 else -((order + 1) // 2))
    return size // 2 + jnp.where(order % 2 == 0, order // 2, -((order + 1) // 2))


def far_step(step):
    return offset(step // 2, ZS), (step + 1) % 2


def near_step(step):
    return offset(step // 4, XS), offset(step % 4, YS)


def exchange_kernel(source_ref, patch_ref, vis_any, weight_any, cell_any, tap_any,
                    got_far, got_near, patches_ref,
                    vis_ref, weight_ref, cell_ref, tap_ref,
                    far_data, near_data, far_middle, near_middle, far_lines, near_lines,
                    far_marks, near_marks, load_sem, local,
                    far_out1, far_in1, near_out1, near_in1, far_out2, far_in2, near_out2, near_in2,
                    far_out3, far_in3, near_out3, near_in3):
    z, x, core, y = position()
    own = GROUP - 1

    loads = []
    for index, (source, target) in enumerate((
            (vis_any, vis_ref), (weight_any, weight_ref), (cell_any, cell_ref), (tap_any, tap_ref))):
        load = pltpu.make_async_copy(source, target.at[pl.ds(0, BLOCKS)], load_sem.at[index])
        load.start()
        loads.append(load)
        target[BLOCKS:] = jnp.zeros_like(target[BLOCKS:])

    def far_device(step):
        dz, dc = far_step(step)
        return ((((z + dz) % ZS) * XS + x) * CORES + (core + dc) % CORES, y)

    def near_device(step):
        dx, dy = near_step(step)
        return ((z * XS + (x + dx) % XS) * CORES + core, (y + dy) % YS)

    barrier = pltpu.get_barrier_semaphore()
    for step in range(own):
        pl.semaphore_signal(barrier, inc=1, device_id=far_device(step), device_id_type=MESH)
        pl.semaphore_signal(barrier, inc=1, device_id=near_device(step), device_id_type=MESH)
    for load in loads:
        load.wait()

    lane = lax.broadcasted_iota(i32, (1, 128), 1)

    def fill(data, slot, first):
        def line(number, carry):
            marks = jnp.zeros((1, 128), i32)
            for k in range(8):
                second = number * 8 + k
                block = source_ref[slot, first * GROUP + second if slot == 0 else second * GROUP + first]
                weight = weight_ref[pl.ds(block, 1), :]
                data[first, 3 * second] = vis_ref[block, 0:1, :] * weight
                data[first, 3 * second + 1] = vis_ref[block, 1:2, :] * weight
                code = cell_ref[pl.ds(block, 1), :] * (OVER * OVER) + tap_ref[pl.ds(block, 1), :]
                data[first, 3 * second + 2] = code.astype(f32)
                patch = patch_ref[jnp.minimum(block, BLOCKS - 1)]
                marks = jnp.where(lane == first + GROUP * k, patch, marks)
            data[first, 3 * GROUP + number] = marks.astype(f32)
            return carry

        lax.fori_loop(0, 2, line, 0)

    def send(source, target, out_sem, in_sem, index, device):
        copy = pltpu.make_async_remote_copy(
            src_ref=source, dst_ref=target, send_sem=out_sem.at[index], recv_sem=in_sem.at[index],
            device_id=device, device_id_type=MESH)
        copy.start()
        return copy

    def keep(source, target, index):
        copy = pltpu.make_async_copy(source, target, local.at[index])
        copy.start()
        return copy

    far_first, near_first = [], []
    for step in range(GROUP):
        fill(far_data, 0, step)
        if step == 0:
            pl.semaphore_wait(barrier, 2 * own)
        if step < own:
            far_first.append(send(far_data.at[step], far_middle.at[step], far_out1, far_in1, step, far_device(step)))
        else:
            far_first.append(keep(far_data.at[step], far_middle.at[step], 0))
        fill(near_data, 1, step)
        if step < own:
            near_first.append(send(near_data.at[step], near_middle.at[step], near_out1, near_in1, step, near_device(step)))
        else:
            near_first.append(keep(near_data.at[step], near_middle.at[step], 1))

    def arrive(copies, middle, lines):
        for copy in copies[:own]:
            copy.wait_recv()
        copies[own].wait()
        for line in range(2):
            total = middle[0, 3 * GROUP + line]
            for step in range(1, GROUP):
                total = total + middle[step, 3 * GROUP + line]
            lines[line] = total

    def far_second(step):
        part = near_middle.at[:, pl.ds(3 * step, 3)]
        line = near_lines.at[step // 8]
        if step == own:
            return [keep(part, got_near.at[step], 2), keep(line, near_marks.at[step], 3)]
        return [send(part, got_near.at[step], far_out2, far_in2, step, far_device(step)),
                send(line, near_marks.at[step], far_out3, far_in3, step, far_device(step))]

    def near_second(step):
        part = far_middle.at[:, pl.ds(3 * step, 3)]
        line = far_lines.at[step // 8]
        if step == own:
            return [keep(part, got_far.at[step], 4), keep(line, far_marks.at[step], 5)]
        return [send(part, got_far.at[step], near_out2, near_in2, step, near_device(step)),
                send(line, far_marks.at[step], near_out3, near_in3, step, near_device(step))]

    second = []
    arrive(near_first, near_middle, near_lines)
    for step in range(EARLY):
        second += far_second(step)
    arrive(far_first, far_middle, far_lines)
    for step in range(GROUP):
        second += near_second(step)
        if step + EARLY < GROUP:
            second += far_second(step + EARLY)
    for copy in second:
        copy.wait()
    for copy in far_first[:own] + near_first[:own]:
        copy.wait_send()
    for row, marks in ((0, far_marks), (2, near_marks)):
        for line in range(2):
            total = jnp.zeros((1, 128), f32)
            for k in range(8):
                total = jnp.where(lane // GROUP == k, marks[line * 8 + k], total)
            patches_ref[row + line:row + line + 1, :] = total.astype(i32)


def exchange(source, patch_index, visibilities, vis_weight, cell_index, tap_offsets):
    smem, hbm = pl.BlockSpec(memory_space=pltpu.SMEM), pl.BlockSpec(memory_space=pl.ANY)
    got = jax.ShapeDtypeStruct((GROUP, GROUP, 3, 1, 128), f32)
    message = pltpu.VMEM((GROUP, LINES, 1, 128), f32)
    return pl.pallas_call(
        exchange_kernel,
        out_shape=(got, got, jax.ShapeDtypeStruct((4, 128), i32)),
        in_specs=[smem, smem] + [hbm] * 4,
        out_specs=(hbm, hbm, pl.BlockSpec(memory_space=pltpu.VMEM)),
        scratch_shapes=[
            pltpu.VMEM((BLOCKS + 8, 2, 128), f32), pltpu.VMEM((BLOCKS + 8, 128), f32),
            pltpu.VMEM((BLOCKS + 8, 128), i32), pltpu.VMEM((BLOCKS + 8, 128), i32),
            message, message, message, message,
            pltpu.VMEM((2, 1, 128), f32), pltpu.VMEM((2, 1, 128), f32),
            pltpu.VMEM((GROUP, 1, 128), f32), pltpu.VMEM((GROUP, 1, 128), f32),
            pltpu.SemaphoreType.DMA((4,)), pltpu.SemaphoreType.DMA((6,)),
        ] + [pltpu.SemaphoreType.DMA((GROUP,))] * 12,
        compiler_params=pltpu.CompilerParams(
            collective_id=0, has_side_effects=True, vmem_limit_bytes=60 << 20),
    )(source, patch_index, visibilities, vis_weight, cell_index, tap_offsets)


UNROLL = 32
ROWS = 2 * EXT
CHUNKS = 4


def halves(value):
    high = value.astype(bf16).astype(f32)
    rest = value - high
    return (jnp.concatenate([high, high], 0).astype(bf16), jnp.concatenate([rest, rest], 0).astype(bf16))


def contract(left, right):
    return lax.dot_general(left, right, (((1,), (1,)), ((), ())), preferred_element_type=f32)


def grid_kernel(patch_ref, far_any, near_any, table_ref, tile_ref, right_ref, lower_ref, corner_ref,
                total, got, stage, load_sem, stage_sem):
    loads = []
    for slot, source in enumerate((far_any, near_any)):
        load = pltpu.make_async_copy(source, got.at[slot], load_sem.at[slot])
        load.start()
        loads.append(load)

    def clear(k, carry):
        total[pl.ds(k * 4, 4)] = jnp.zeros((4, ROWS, 128), f32)
        return carry

    lax.fori_loop(0, (PATCHES + SIDE) // 4, clear, 0)
    for load in loads:
        load.wait()

    row8 = lax.broadcasted_iota(i32, (8, 128), 0)
    table = table_ref[...]
    zero = jnp.zeros((16, 128), bf16)

    def steps(cell):
        step = (cell + 7 - row8) >> 3
        return jnp.concatenate([step, step - 1], 0).astype(jnp.int16)

    def one(slot, index):
        real = got[slot, index, 0]
        imag = got[slot, index, 1]
        code = jnp.broadcast_to(got[slot, index, 2], (8, 128)).astype(i32)
        cell_u = code >> 14
        cell_v = (code >> 8) & (SUB - 1)
        ku = jnp.take_along_axis(table, ((code >> 1) & 0x78) + ((row8 - cell_u) & 7), axis=1)
        kv = jnp.take_along_axis(table, ((code << 3) & 0x78) + ((row8 - cell_v) & 7), axis=1)
        step_u, step_v = steps(cell_u), steps(cell_v)
        masks_u = [step_u == jnp.int16(2 * t) for t in range(5)]
        masks_v = [step_v == jnp.int16(2 * t) for t in range(5)]

        def rows_u(first, second):
            return jnp.concatenate(
                [jnp.where(mask, value, zero) for value in (first, second) for mask in masks_u], 0)

        def rows_v(value):
            return jnp.concatenate([jnp.where(mask, value, zero) for mask in masks_v], 0)

        v_high, v_rest = halves(kv)
        r_high, r_rest = halves(ku * real)
        i_high, i_rest = halves(ku * imag)
        v_high, v_rest = rows_v(v_high), rows_v(v_rest)
        u_high, u_rest = rows_u(r_high, i_high), rows_u(r_rest, i_rest)
        out = contract(jnp.concatenate([u_high, u_rest, u_high], 1),
                       jnp.concatenate([v_high, v_high, v_rest], 1))
        patch = patch_ref[2 * slot + index // 128, index % 128] + SIDE
        total[patch, 0:EXT, 0:80] = total[patch, 0:EXT, 0:80] + out[0:EXT]
        total[patch, EXT:ROWS, 0:80] = total[patch, EXT:ROWS, 0:80] + out[80:80 + EXT]

    def several(k, carry):
        for q in range(UNROLL):
            for slot in range(2):
                one(slot, k * UNROLL + q)
        return carry

    lax.fori_loop(0, BLOCKS // UNROLL, several, 0)

    lane = lax.broadcasted_iota(i32, (8, 128), 1)
    right_ref[...] = jnp.zeros_like(right_ref)

    def joined(load, put):
        before = jnp.zeros((8, 128), f32)
        for pair in range(SIDE // 2):
            moved = pltpu.roll(load(2 * pair + 1), SUB, 1)
            put(pair, load(2 * pair) + jnp.where(lane >= SUB, moved, before))
            before = moved
        return jnp.where(lane < KW, before, 0.0)

    def stripe(patch_row):
        for part in range(2):
            for step in range(SUB // 8):
                start = part * EXT + step * 8

                def load(column):
                    value = total[(patch_row + 1) * SIDE + column, start:start + 8, :]
                    if step == 0:
                        last = part * EXT + SUB
                        value = value + total[patch_row * SIDE + column, last:last + 8, :]
                    return value

                def put(pair, value):
                    place = pl.multiple_of(patch_row * SUB + step * 8, 8)
                    stage[part, pl.ds(place, 8), pair * 128:pair * 128 + 128] = value

                past = joined(load, put)
                rows = slice(step * 8, step * 8 + 8)
                right_ref[part, rows, :] = right_ref[part, rows, :] + pltpu.roll(past, patch_row * KW, 1)

    def each(patch_row, carry):
        stripe(patch_row)
        for part in range(2):
            for chunk in range(CHUNKS):
                rows = pl.ds(patch_row * SUB + chunk * (SUB // CHUNKS), SUB // CHUNKS)
                pltpu.make_async_copy(stage.at[part, rows], tile_ref.at[part, rows], stage_sem).start()
        return carry

    lax.fori_loop(0, SIDE, each, 0)

    for part in range(2):
        last = part * EXT + SUB

        def load(column):
            return total[SIDE * SIDE + column, last:last + 8, :]

        def put(pair, value):
            lower_ref[part, :, pair * 128:pair * 128 + 128] = value

        corner_ref[part] = joined(load, put)
    pltpu.make_async_copy(stage, tile_ref, stage_sem).wait()


def make_tile(patches, far, near, table):
    vmem, hbm = pl.BlockSpec(memory_space=pltpu.VMEM), pl.BlockSpec(memory_space=pl.ANY)
    return pl.pallas_call(
        grid_kernel,
        out_shape=(
            jax.ShapeDtypeStruct((2, TILE, TILE), f32), jax.ShapeDtypeStruct((2, SUB, 128), f32),
            jax.ShapeDtypeStruct((2, KW, TILE), f32), jax.ShapeDtypeStruct((2, KW, 128), f32)),
        in_specs=[pl.BlockSpec(memory_space=pltpu.SMEM), hbm, hbm, vmem],
        out_specs=(hbm, vmem, vmem, vmem),
        scratch_shapes=[
            pltpu.VMEM((PATCHES + SIDE, ROWS, 128), f32),
            pltpu.VMEM((2, BLOCKS, 3, 1, 128), f32),
            pltpu.VMEM((2, TILE, TILE), f32),
            pltpu.SemaphoreType.DMA((2,)), pltpu.SemaphoreType.DMA,
        ],
        compiler_params=pltpu.CompilerParams(vmem_limit_bytes=60 << 20),
    )(patches, far, near, table)


def margins_kernel(right_ref, lower_ref, corner_ref, left_in, upper_in, corner_in, out_sem, in_sem):
    tile, y = lax.axis_index("tile"), lax.axis_index("wp")
    tiles = ZS * XS * CORES
    barrier = pltpu.get_barrier_semaphore()
    steps = (1, TCOLS, TCOLS + 1)
    for step in steps:
        for to in ((tile + step) % tiles, (tile + tiles - step) % tiles):
            pl.semaphore_signal(barrier, inc=1, device_id=(to, y), device_id_type=MESH)
    pl.semaphore_wait(barrier, 2 * len(steps))
    copies = []
    for index, (source, target) in enumerate(
            ((right_ref, left_in), (lower_ref, upper_in), (corner_ref, corner_in))):
        copy = pltpu.make_async_remote_copy(
            src_ref=source, dst_ref=target, send_sem=out_sem.at[index], recv_sem=in_sem.at[index],
            device_id=((tile + steps[index]) % tiles, y), device_id_type=MESH)
        copy.start()
        copies.append(copy)
    for copy in copies:
        copy.wait()


def margins(right, lower, corner):
    hbm = pl.BlockSpec(memory_space=pl.ANY)
    return pl.pallas_call(
        margins_kernel,
        out_shape=tuple(jax.ShapeDtypeStruct(a.shape, a.dtype) for a in (right, lower, corner)),
        in_specs=[hbm] * 3,
        out_specs=(hbm,) * 3,
        scratch_shapes=[pltpu.SemaphoreType.DMA((3,)), pltpu.SemaphoreType.DMA((3,))],
        compiler_params=pltpu.CompilerParams(collective_id=1, has_side_effects=True, vmem_limit_bytes=60 << 20),
    )(right, lower, corner)


def finish_kernel(tile_in, left_any, upper_any, corner_any, tile_ref,
                  side, top, left_in, upper_in, corner_in, sems):
    del tile_in
    tile = lax.axis_index("tile")
    has_left = jnp.where(tile % TCOLS > 0, 1.0, 0.0).astype(f32)
    has_upper = jnp.where(tile // TCOLS > 0, 1.0, 0.0).astype(f32)
    sides = tile_ref.at[:, :, pl.ds(0, 128)]
    tops = tile_ref.at[:, pl.ds(0, KW), pl.ds(128, TILE - 128)]
    read_side = pltpu.make_async_copy(sides, side, sems.at[0])
    read_top = pltpu.make_async_copy(tops, top, sems.at[1])
    read_side.start()
    read_top.start()
    loads = []
    for index, (source, target) in enumerate(
            ((upper_any, upper_in), (left_any, left_in), (corner_any, corner_in))):
        load = pltpu.make_async_copy(source, target, sems.at[2 + index])
        load.start()
        loads.append(load)
    lane = lax.broadcasted_iota(i32, (SUB, 128), 1)
    read_top.wait()
    loads[0].wait()
    top[...] = top[...] + upper_in[:, :, 128:] * has_upper
    write_top = pltpu.make_async_copy(top, tops, sems.at[1])
    write_top.start()
    read_side.wait()
    loads[1].wait()
    loads[2].wait()
    for part in range(2):
        packed = left_in[part] * has_left
        for patch_row in range(SIDE):
            rows = slice(patch_row * SUB, patch_row * SUB + SUB)
            moved = packed if patch_row == 0 else pltpu.roll(packed, 128 - KW * patch_row, 1)
            side[part, rows, :] = side[part, rows, :] + jnp.where(lane < KW, moved, 0.0)
        side[part, 0:KW, :] = (side[part, 0:KW, :] + upper_in[part, :, 0:128] * has_upper
                               + corner_in[part] * (has_left * has_upper))
    write_side = pltpu.make_async_copy(side, sides, sems.at[0])
    write_side.start()
    write_top.wait()
    write_side.wait()


def finish(tile, left, upper, corner):
    hbm = pl.BlockSpec(memory_space=pl.ANY)
    return pl.pallas_call(
        finish_kernel,
        out_shape=jax.ShapeDtypeStruct(tile.shape, tile.dtype),
        in_specs=[hbm] * 4,
        out_specs=hbm,
        scratch_shapes=[
            pltpu.VMEM((2, TILE, 128), f32), pltpu.VMEM((2, KW, TILE - 128), f32),
            pltpu.VMEM(left.shape, f32), pltpu.VMEM(upper.shape, f32), pltpu.VMEM(corner.shape, f32),
            pltpu.SemaphoreType.DMA((5,))],
        input_output_aliases={0: 0},
        compiler_params=pltpu.CompilerParams(vmem_limit_bytes=60 << 20),
    )(tile, left, upper, corner)


def shards(visibilities, vis_weight, cell_index, tap_offsets, routes, patch_index, kernel):
    blocks = visibilities.shape[0]
    block_ids = lax.broadcasted_iota(i32, (blocks, blocks), 0)
    step = lax.broadcasted_iota(i32, (blocks, blocks), 1)
    z, x, core, y = position()
    (dz, dc), (dx, dy) = far_step(step // GROUP), near_step(step % GROUP)
    target = ((((z + dz) % ZS) * XS + (x + dx) % XS) * CORES + (core + dc) % CORES) * YS + (y + dy) % YS
    named = routes == target
    first = jnp.min(jnp.where(named, block_ids, blocks), axis=0)
    last = jnp.max(jnp.where(named, block_ids, -1), axis=0)
    source = jnp.stack([first, jnp.where(last > first, last, blocks)])
    far, near, patches = exchange(source, patch_index, visibilities, vis_weight, cell_index, tap_offsets)
    table = jnp.broadcast_to(kernel.reshape(1, OVER * KW), (8, OVER * KW))
    tile, right, lower, corner = make_tile(
        patches, far.reshape(BLOCKS, 3, 1, 128), near.reshape(BLOCKS, 3, 1, 128), table)
    tile = finish(tile, *margins(right, lower, corner))
    return tile.reshape(1, 1, 2, TILE, TILE)


def solution(mesh):
    in_specs = (
        P(("tile", "wp"), None, None),
        P(("tile", "wp"), None),
        P(("tile", "wp"), None),
        P(("tile", "wp"), None),
        P(("tile", "wp"), None),
        P(("tile", "wp")),
        P(),
    )
    out_specs = P("wp", "tile", None, None, None)
    return jax.shard_map(shards, mesh=mesh, in_specs=in_specs, out_specs=out_specs, check_vma=False)
```

time: 102 us -> 75.3 us (0.74)
  Pallas kernels: 90.6 us -> 72.1 us
  local copies, waits for them, and re-layouts: 9.4 us -> 1.44 us
    pallas_call x1, Pallas kernels: 44.6 us -> 32.1 us  [exchange(): pl.pallas_call(exchange_kernel, out_shape=(got, got, jax.ShapeDtypeStruct...]
    unnamed x23 -> x1, local copies, waits for them, and re-layouts: 9.31 us -> 0.76 us
    pallas_call x1, Pallas kernels: 31.8 us -> 28.1 us  [make_tile(): pl.pallas_call(grid_kernel, out_shape=(jax.ShapeDtypeStruct((2, TILE, TIL...]
    pallas_call x1, Pallas kernels: 11.6 us -> 9.27 us  [margins(): pl.pallas_call(margins_kernel, out_shape=tuple((jax.ShapeDtypeStruct(a.sh...]
where the time goes in v2:
time: 75.3 us; the launch traced here: 75.1 us
  Pallas kernels  72.1 us (96%)
  other arithmetic  1.44 us (2%)
  local copies, waits for them, and re-layouts  1.44 us (2%)
    pallas_call x1, Pallas kernels, exchange(): pl.pallas_call(exchange_kernel, out_shape=(got, got, jax.ShapeDtypeStruct...  32.1 us
    pallas_call x1, Pallas kernels, make_tile(): pl.pallas_call(grid_kernel, out_shape=(jax.ShapeDtypeStruct((2, TILE, TIL...  28.1 us
    pallas_call x1, Pallas kernels, margins(): pl.pallas_call(margins_kernel, out_shape=tuple((jax.ShapeDtypeStruct(a.sh...  9.27 us
    pallas_call x1, Pallas kernels, finish(): pl.pallas_call(finish_kernel, out_shape=jax.ShapeDtypeStruct(tile.shape,...  2.57 us

profile of v2, /device:TPU:8, one launch (start us, length us, event | category | flops | bytes accessed | tf_op | source)
XLA Modules:
  0.0 75.1 jit_solution(8186748982598308376)
XLA Ops:
  0.0 0.8 %select_reduce_fusion.1 = (s32[256]{0:T(256)S(1)}, s32[256]{0:T(256)S(1)}) fusion(s32[]{:T(128)S(6)} %axis_index.25, s32[]{:T(128)S(6)} %select_n.137, s32[256]{0:T(256)S(1)} %get-tuple-element.28, s32[256]{0:T(256)S(1)} %get-tuple-element.31, pred[256]{0:T(512)(128)(4,1)S(1)} %get-tuple-element.29, s32[]{:T(128)S(6)} %select_n.129, ...), kind=kLoop, calls=%fused_computation.99 | loop fusion | flops 14679552 | bytes 7696 | tf_op jit(solution)/shard_map/reduce_min | solution.py:443
  0.9 0.6 pad_add_fusion.source_ref
  1.5 0.8 %copy.11 = f32[16,8]{1,0:T(8,128)S(1)} copy(f32[16,8]{0,1:T(8,128)} %param.13) | data formatting | bytes 1024 | tf_op args[6]
  2.2 0.1 broadcast_in_dim.18
  2.3 0.6 broadcast_in_dim.19.table_ref
  2.9 32.1 %shard_map.73 = (f32[16,16,3,1,128]{4,3,2,1,0:T(1,128)}, f32[16,16,3,1,128]{4,3,2,1,0:T(1,128)}, s32[4,128]{1,0:T(4,128)}) custom-call(s32[2,256]{1,0:T(2,128)} %pad_add_fusion.source_ref, s32[256]{0:T(256)} %patch_ref.1, f32[256,2,128]{2,1,0:T(2,128)} %vis_any.1, f32[256,128]{1,0:T(8,128)} %weight_any.1, s32[256,128]{1,0:T(8,128)} %cell_any.1, ...), custom_call_target="tpu_custom_call" | custom-call | tf_op jit(solution)/shard_map/pallas_call | solution.py:177
  35.0 28.1 %shard_map.74 = (f32[2,1024,1024]{2,1,0:T(8,128)}, f32[2,64,128]{2,1,0:T(8,128)}, f32[2,8,1024]{2,1,0:T(8,128)}, f32[2,8,128]{2,1,0:T(8,128)}) custom-call(s32[4,128]{1,0:T(4,128)} %get-tuple-element.15.patch_ref, f32[256,3,1,128]{3,2,1,0:T(1,128)} %bitcast.6, f32[256,3,1,128]{3,2,1,0:T(1,128)} %bitcast.7, f32[8,128]{1,0:T(8,128)} %broadcast_in_dim.19.table_ref), custom_call_target="tpu_custom_call" | custom-call | tf_op jit(solution)/shard_map/pallas_call | solution.py:328
  63.2 9.3 %shard_map.75 = (f32[2,64,128]{2,1,0:T(8,128)}, f32[2,8,1024]{2,1,0:T(8,128)}, f32[2,8,128]{2,1,0:T(8,128)}) custom-call(f32[2,64,128]{2,1,0:T(8,128)} %get-tuple-element.19.right_ref, f32[2,8,1024]{2,1,0:T(8,128)} %get-tuple-element.20.lower_ref, f32[2,8,128]{2,1,0:T(8,128)} %get-tuple-element.21.corner_ref), custom_call_target="tpu_custom_call" | custom-call | tf_op jit(solution)/shard_map/pallas_call | solution.py:368
  72.5 2.6 %shard_map.76 = f32[2,1024,1024]{2,1,0:T(8,128)} custom-call(f32[2,1024,1024]{2,1,0:T(8,128)} %get-tuple-element.18.tile_in, f32[2,64,128]{2,1,0:T(8,128)} %get-tuple-element.22.left_any, f32[2,8,1024]{2,1,0:T(8,128)} %get-tuple-element.23.upper_any, f32[2,8,128]{2,1,0:T(8,128)} %get-tuple-element.24.corner_any), custom_call_target="tpu_custom_call", output_to_operand_aliasing={{}: (0, {})} | custom-call | tf_op jit(solution)/shard_map/pallas_call | solution.py:421
  (4 shorter events, 0.0 us)

commit v3 on v2

--- a/solution.py
+++ b/solution.py
@@ -192,7 +192,8 @@
     )(source, patch_index, visibilities, vis_weight, cell_index, tap_offsets)
 
 
-UNROLL = 32
+UNROLL = 64
+SLOTS = 2 * BLOCKS
 ROWS = 2 * EXT
 CHUNKS = 4
 
@@ -207,34 +208,63 @@
     return lax.dot_general(left, right, (((1,), (1,)), ((), ())), preferred_element_type=f32)
 
 
-def grid_kernel(patch_ref, far_any, near_any, table_ref, tile_ref, right_ref, lower_ref, corner_ref,
-                total, got, stage, load_sem, stage_sem):
+def column(row):
+    return jnp.transpose(jnp.broadcast_to(row, (128, 128)))
+
+
+def grid_kernel(patch_ref, far_any, near_any, taps_ref, tile_ref, right_ref, lower_ref, corner_ref,
+                total, got, stage, beyond, sorted_rows, sorted_keys, taps, load_sem, stage_sem):
     loads = []
     for slot, source in enumerate((far_any, near_any)):
-        load = pltpu.make_async_copy(source, got.at[slot], load_sem.at[slot])
+        load = pltpu.make_async_copy(source, got.at[pl.ds(slot * BLOCKS, BLOCKS)], load_sem.at[slot])
         load.start()
         loads.append(load)
+
+    lane = lax.broadcasted_iota(i32, (1, 128), 1)
+    keys = [(patch_ref[c:c + 1, :] * SLOTS + (lane + 128 * c)).astype(f32) for c in range(4)]
+    key_columns = [column(key) for key in keys]
+    ranks = []
+    for key in keys:
+        below = [jnp.where(other < key, 1.0, 0.0) for other in key_columns]
+        ranks.append(jnp.sum(below[0] + below[1] + below[2] + below[3], axis=0, keepdims=True))
+    rank_columns = [column(rank) for rank in ranks]
+    for c in range(4):
+        place = (lane + 128 * c).astype(f32)
+        here = [jnp.where(rank_columns[d] == place, key_columns[d], 0.0) for d in range(4)]
+        chosen = jnp.sum(here[0] + here[1] + here[2] + here[3], axis=0, keepdims=True)
+        sorted_rows[c:c + 1, :] = chosen.astype(i32)
+    load = pltpu.make_async_copy(sorted_rows, sorted_keys, load_sem.at[2])
+    load.start()
+    loads.append(load)
 
     def clear(k, carry):
         total[pl.ds(k * 4, 4)] = jnp.zeros((4, ROWS, 128), f32)
         return carry
 
     lax.fori_loop(0, (PATCHES + SIDE) // 4, clear, 0)
+
+    taps[...] = jnp.zeros_like(taps)
+    taps[:, 0:OVER] = taps_ref[...]
+    wide = lax.broadcasted_iota(i32, (8, 128), 1)
+    spread = jnp.take_along_axis(taps[...], wide // KW, axis=1)
+    own = lax.broadcasted_iota(i32, (8, 128), 0) == wide % KW
+    table = jnp.broadcast_to(jnp.sum(jnp.where(own, spread, 0.0), axis=0, keepdims=True), (8, 128))
+
     for load in loads:
         load.wait()
 
     row8 = lax.broadcasted_iota(i32, (8, 128), 0)
-    table = table_ref[...]
     zero = jnp.zeros((16, 128), bf16)
 
     def steps(cell):
         step = (cell + 7 - row8) >> 3
         return jnp.concatenate([step, step - 1], 0).astype(jnp.int16)
 
-    def one(slot, index):
-        real = got[slot, index, 0]
-        imag = got[slot, index, 1]
-        code = jnp.broadcast_to(got[slot, index, 2], (8, 128)).astype(i32)
+    def one(key):
+        block = key % SLOTS
+        real = got[block, 0]
+        imag = got[block, 1]
+        code = jnp.broadcast_to(got[block, 2], (8, 128)).astype(i32)
         cell_u = code >> 14
         cell_v = (code >> 8) & (SUB - 1)
         ku = jnp.take_along_axis(table, ((code >> 1) & 0x78) + ((row8 - cell_u) & 7), axis=1)
@@ -257,20 +287,11 @@
         u_high, u_rest = rows_u(r_high, i_high), rows_u(r_rest, i_rest)
         out = contract(jnp.concatenate([u_high, u_rest, u_high], 1),
                        jnp.concatenate([v_high, v_high, v_rest], 1))
-        patch = patch_ref[2 * slot + index // 128, index % 128] + SIDE
+        patch = key // SLOTS + SIDE
         total[patch, 0:EXT, 0:80] = total[patch, 0:EXT, 0:80] + out[0:EXT]
         total[patch, EXT:ROWS, 0:80] = total[patch, EXT:ROWS, 0:80] + out[80:80 + EXT]
 
-    def several(k, carry):
-        for q in range(UNROLL):
-            for slot in range(2):
-                one(slot, k * UNROLL + q)
-        return carry
-
-    lax.fori_loop(0, BLOCKS // UNROLL, several, 0)
-
     lane = lax.broadcasted_iota(i32, (8, 128), 1)
-    right_ref[...] = jnp.zeros_like(right_ref)
 
     def joined(load, put):
         before = jnp.zeros((8, 128), f32)
@@ -297,8 +318,7 @@
                     stage[part, pl.ds(place, 8), pair * 128:pair * 128 + 128] = value
 
                 past = joined(load, put)
-                rows = slice(step * 8, step * 8 + 8)
-                right_ref[part, rows, :] = right_ref[part, rows, :] + pltpu.roll(past, patch_row * KW, 1)
+                beyond[patch_row, part, step * 8:step * 8 + 8, :] = past
 
     def each(patch_row, carry):
         stripe(patch_row)
@@ -308,7 +328,18 @@
                 pltpu.make_async_copy(stage.at[part, rows], tile_ref.at[part, rows], stage_sem).start()
         return carry
 
-    lax.fori_loop(0, SIDE, each, 0)
+    def key_at(position):
+        return sorted_keys[position // 128, position % 128]
+
+    def several(k, done):
+        for q in range(UNROLL):
+            one(key_at(k * UNROLL + q))
+        following = key_at(jnp.minimum((k + 1) * UNROLL, SLOTS - 1)) // (SLOTS * SIDE)
+        ready = jnp.where(k == SLOTS // UNROLL - 1, SIDE, following)
+        lax.fori_loop(done, ready, each, 0)
+        return ready
+
+    lax.fori_loop(0, SLOTS // UNROLL, several, 0)
 
     for part in range(2):
         last = part * EXT + SUB
@@ -320,26 +351,35 @@
             lower_ref[part, :, pair * 128:pair * 128 + 128] = value
 
         corner_ref[part] = joined(load, put)
+    for part in range(2):
+        for step in range(SUB // 8):
+            rows = slice(step * 8, step * 8 + 8)
+            packed = beyond[0, part, rows, :]
+            for patch_row in range(1, SIDE):
+                packed = packed + pltpu.roll(beyond[patch_row, part, rows, :], patch_row * KW, 1)
+            right_ref[part, rows, :] = packed
     pltpu.make_async_copy(stage, tile_ref, stage_sem).wait()
 
 
-def make_tile(patches, far, near, table):
+def make_tile(patches, far, near, taps):
     vmem, hbm = pl.BlockSpec(memory_space=pltpu.VMEM), pl.BlockSpec(memory_space=pl.ANY)
     return pl.pallas_call(
         grid_kernel,
         out_shape=(
             jax.ShapeDtypeStruct((2, TILE, TILE), f32), jax.ShapeDtypeStruct((2, SUB, 128), f32),
             jax.ShapeDtypeStruct((2, KW, TILE), f32), jax.ShapeDtypeStruct((2, KW, 128), f32)),
-        in_specs=[pl.BlockSpec(memory_space=pltpu.SMEM), hbm, hbm, vmem],
+        in_specs=[vmem, hbm, hbm, vmem],
         out_specs=(hbm, vmem, vmem, vmem),
         scratch_shapes=[
             pltpu.VMEM((PATCHES + SIDE, ROWS, 128), f32),
-            pltpu.VMEM((2, BLOCKS, 3, 1, 128), f32),
+            pltpu.VMEM((SLOTS, 3, 1, 128), f32),
             pltpu.VMEM((2, TILE, TILE), f32),
-            pltpu.SemaphoreType.DMA((2,)), pltpu.SemaphoreType.DMA,
+            pltpu.VMEM((SIDE, 2, SUB, 128), f32),
+            pltpu.VMEM((4, 128), i32), pltpu.SMEM((4, 128), i32), pltpu.VMEM((KW, 128), f32),
+            pltpu.SemaphoreType.DMA((3,)), pltpu.SemaphoreType.DMA,
         ],
         compiler_params=pltpu.CompilerParams(vmem_limit_bytes=60 << 20),
-    )(patches, far, near, table)
+    )(patches, far, near, taps)
 
 
 def margins_kernel(right_ref, lower_ref, corner_ref, left_in, upper_in, corner_in, out_sem, in_sem):
@@ -444,9 +484,8 @@
     last = jnp.max(jnp.where(named, block_ids, -1), axis=0)
     source = jnp.stack([first, jnp.where(last > first, last, blocks)])
     far, near, patches = exchange(source, patch_index, visibilities, vis_weight, cell_index, tap_offsets)
-    table = jnp.broadcast_to(kernel.reshape(1, OVER * KW), (8, OVER * KW))
     tile, right, lower, corner = make_tile(
-        patches, far.reshape(BLOCKS, 3, 1, 128), near.reshape(BLOCKS, 3, 1, 128), table)
+        patches, far.reshape(BLOCKS, 3, 1, 128), near.reshape(BLOCKS, 3, 1, 128), kernel.T)
     tile = finish(tile, *margins(right, lower, corner))
     return tile.reshape(1, 1, 2, TILE, TILE)
 

time: 75.3 us -> 71.5 us (0.950)
  Pallas kernels: 72.1 us -> 69.8 us
  local copies, waits for them, and re-layouts: 1.44 us -> 0 us
    pallas_call x1, Pallas kernels: 28.1 us -> 25.8 us  [make_tile(): pl.pallas_call(grid_kernel, out_shape=(jax.ShapeDtypeStruct((2, TILE, TIL...]
    unnamed x1 -> x0, local copies, waits for them, and re-layouts: 0.76 us -> none
where the time goes in v3:
time: 71.5 us; the launch traced here: 71.3 us
  Pallas kernels  69.8 us (98%)
  other arithmetic  1.44 us (2%)
    pallas_call x1, Pallas kernels, exchange(): pl.pallas_call(exchange_kernel, out_shape=(got, got, jax.ShapeDtypeStruct...  32.1 us
    pallas_call x1, Pallas kernels, make_tile(): pl.pallas_call(grid_kernel, out_shape=(jax.ShapeDtypeStruct((2, TILE, TIL...  25.8 us
    pallas_call x1, Pallas kernels, margins(): pl.pallas_call(margins_kernel, out_shape=tuple((jax.ShapeDtypeStruct(a.sh...  9.27 us
    pallas_call x1, Pallas kernels, finish(): pl.pallas_call(finish_kernel, out_shape=jax.ShapeDtypeStruct(tile.shape,...  2.57 us

profile of v3, /device:TPU:8, one launch (start us, length us, event | category | flops | bytes accessed | tf_op | source)
XLA Modules:
  0.0 71.3 jit_solution(7446937526022458427)
XLA Ops:
  0.0 0.8 %select_reduce_fusion.1 = (s32[256]{0:T(256)S(1)}, s32[256]{0:T(256)S(1)}) fusion(s32[]{:T(128)S(6)} %axis_index.25, s32[]{:T(128)S(6)} %select_n.137, s32[256]{0:T(256)S(1)} %get-tuple-element.28, s32[256]{0:T(256)S(1)} %get-tuple-element.31, pred[256]{0:T(512)(128)(4,1)S(1)} %get-tuple-element.29, s32[]{:T(128)S(6)} %select_n.129, ...), kind=kLoop, calls=%fused_computation.99 | loop fusion | flops 14679552 | bytes 7696 | tf_op jit(solution)/shard_map/reduce_min | solution.py:483
  0.9 0.6 pad_add_fusion.source_ref
  1.5 32.1 %shard_map.73 = (f32[16,16,3,1,128]{4,3,2,1,0:T(1,128)}, f32[16,16,3,1,128]{4,3,2,1,0:T(1,128)}, s32[4,128]{1,0:T(4,128)}) custom-call(s32[2,256]{1,0:T(2,128)} %pad_add_fusion.source_ref, s32[256]{0:T(256)} %patch_ref.1, f32[256,2,128]{2,1,0:T(2,128)} %vis_any.1, f32[256,128]{1,0:T(8,128)} %weight_any.1, s32[256,128]{1,0:T(8,128)} %cell_any.1, ...), custom_call_target="tpu_custom_call" | custom-call | tf_op jit(solution)/shard_map/pallas_call | solution.py:177
  33.6 25.8 %shard_map.74 = (f32[2,1024,1024]{2,1,0:T(8,128)}, f32[2,64,128]{2,1,0:T(8,128)}, f32[2,8,1024]{2,1,0:T(8,128)}, f32[2,8,128]{2,1,0:T(8,128)}) custom-call(s32[4,128]{1,0:T(4,128)} %get-tuple-element.15.patch_ref, f32[256,3,1,128]{3,2,1,0:T(1,128)} %bitcast.7, f32[256,3,1,128]{3,2,1,0:T(1,128)} %bitcast.8, f32[8,16]{1,0:T(8,128)} %bitcast.9), custom_call_target="tpu_custom_call" | custom-call | tf_op jit(solution)/shard_map/pallas_call | solution.py:366
  59.4 9.3 %shard_map.75 = (f32[2,64,128]{2,1,0:T(8,128)}, f32[2,8,1024]{2,1,0:T(8,128)}, f32[2,8,128]{2,1,0:T(8,128)}) custom-call(f32[2,64,128]{2,1,0:T(8,128)} %get-tuple-element.19.right_ref, f32[2,8,1024]{2,1,0:T(8,128)} %get-tuple-element.20.lower_ref, f32[2,8,128]{2,1,0:T(8,128)} %get-tuple-element.21.corner_ref), custom_call_target="tpu_custom_call" | custom-call | tf_op jit(solution)/shard_map/pallas_call | solution.py:408
  68.7 2.6 %shard_map.76 = f32[2,1024,1024]{2,1,0:T(8,128)} custom-call(f32[2,1024,1024]{2,1,0:T(8,128)} %get-tuple-element.18.tile_in, f32[2,64,128]{2,1,0:T(8,128)} %get-tuple-element.22.left_any, f32[2,8,1024]{2,1,0:T(8,128)} %get-tuple-element.23.upper_any, f32[2,8,128]{2,1,0:T(8,128)} %get-tuple-element.24.corner_any), custom_call_target="tpu_custom_call", output_to_operand_aliasing={{}: (0, {})} | custom-call | tf_op jit(solution)/shard_map/pallas_call | solution.py:461
  (4 shorter events, 0.0 us)

commit v4 on v3

--- a/solution.py
+++ b/solution.py
@@ -43,9 +43,9 @@
     return offset(step // 4, XS), offset(step % 4, YS)
 
 
-def exchange_kernel(source_ref, patch_ref, vis_any, weight_any, cell_any, tap_any,
+def exchange_kernel(patch_ref, routes_any, vis_any, weight_any, cell_any, tap_any,
                     got_far, got_near, patches_ref,
-                    vis_ref, weight_ref, cell_ref, tap_ref,
+                    vis_ref, weight_ref, cell_ref, tap_ref, routes_ref, source_rows, source_ref,
                     far_data, near_data, far_middle, near_middle, far_lines, near_lines,
                     far_marks, near_marks, load_sem, local,
                     far_out1, far_in1, near_out1, near_in1, far_out2, far_in2, near_out2, near_in2,
@@ -61,6 +61,9 @@
         loads.append(load)
         target[BLOCKS:] = jnp.zeros_like(target[BLOCKS:])
 
+    route_load = pltpu.make_async_copy(routes_any, routes_ref, load_sem.at[4])
+    route_load.start()
+
     def far_device(step):
         dz, dc = far_step(step)
         return ((((z + dz) % ZS) * XS + x) * CORES + (core + dc) % CORES, y)
@@ -73,17 +76,39 @@
     for step in range(own):
         pl.semaphore_signal(barrier, inc=1, device_id=far_device(step), device_id_type=MESH)
         pl.semaphore_signal(barrier, inc=1, device_id=near_device(step), device_id_type=MESH)
+    lane = lax.broadcasted_iota(i32, (1, 128), 1)
+    route_load.wait()
+    row = lax.broadcasted_iota(i32, (128, 128), 0)
+    columns = [jnp.transpose(jnp.broadcast_to(routes_ref[:, 128 * d:128 * d + 128], (128, 128))) for d in range(2)]
+
+    def ring(order, size):
+        return size // 2 + jnp.where(order & 1 == 0, order >> 1, -((order + 1) >> 1))
+
+    for c in range(2):
+        step = lane + 128 * c
+        far, near = step >> 4, step & (GROUP - 1)
+        to_z, to_core = (z + ring(far >> 1, ZS)) & (ZS - 1), (core + far + 1) & (CORES - 1)
+        to_x, to_y = (x + ring(near >> 2, XS)) & (XS - 1), (y + ring(near & (YS - 1), YS)) & (YS - 1)
+        target = ((to_z * XS + to_x) * CORES + to_core) * YS + to_y
+        named = [column == target for column in columns]
+        first = jnp.minimum(jnp.where(named[0], row, BLOCKS), jnp.where(named[1], row + 128, BLOCKS))
+        last = jnp.maximum(jnp.where(named[0], row, -1), jnp.where(named[1], row + 128, -1))
+        first, last = jnp.min(first, axis=0, keepdims=True), jnp.max(last, axis=0, keepdims=True)
+        source_rows[c:c + 1, :] = first
+        source_rows[2 + c:3 + c, :] = jnp.where(last > first, last, BLOCKS)
+    numbers = pltpu.make_async_copy(source_rows, source_ref, load_sem.at[5])
+    numbers.start()
     for load in loads:
         load.wait()
-
-    lane = lax.broadcasted_iota(i32, (1, 128), 1)
+    numbers.wait()
 
     def fill(data, slot, first):
         def line(number, carry):
             marks = jnp.zeros((1, 128), i32)
             for k in range(8):
                 second = number * 8 + k
-                block = source_ref[slot, first * GROUP + second if slot == 0 else second * GROUP + first]
+                step = first * GROUP + second if slot == 0 else second * GROUP + first
+                block = source_ref[2 * slot + step // 128, step % 128]
                 weight = weight_ref[pl.ds(block, 1), :]
                 data[first, 3 * second] = vis_ref[block, 0:1, :] * weight
                 data[first, 3 * second + 1] = vis_ref[block, 1:2, :] * weight
@@ -170,26 +195,27 @@
             patches_ref[row + line:row + line + 1, :] = total.astype(i32)
 
 
-def exchange(source, patch_index, visibilities, vis_weight, cell_index, tap_offsets):
+def exchange(patch_index, routes, visibilities, vis_weight, cell_index, tap_offsets):
     smem, hbm = pl.BlockSpec(memory_space=pltpu.SMEM), pl.BlockSpec(memory_space=pl.ANY)
     got = jax.ShapeDtypeStruct((GROUP, GROUP, 3, 1, 128), f32)
     message = pltpu.VMEM((GROUP, LINES, 1, 128), f32)
     return pl.pallas_call(
         exchange_kernel,
         out_shape=(got, got, jax.ShapeDtypeStruct((4, 128), i32)),
-        in_specs=[smem, smem] + [hbm] * 4,
+        in_specs=[smem] + [hbm] * 5,
         out_specs=(hbm, hbm, pl.BlockSpec(memory_space=pltpu.VMEM)),
         scratch_shapes=[
             pltpu.VMEM((BLOCKS + 8, 2, 128), f32), pltpu.VMEM((BLOCKS + 8, 128), f32),
             pltpu.VMEM((BLOCKS + 8, 128), i32), pltpu.VMEM((BLOCKS + 8, 128), i32),
+            pltpu.VMEM((1, BLOCKS), i32), pltpu.VMEM((4, 128), i32), pltpu.SMEM((4, 128), i32),
             message, message, message, message,
             pltpu.VMEM((2, 1, 128), f32), pltpu.VMEM((2, 1, 128), f32),
             pltpu.VMEM((GROUP, 1, 128), f32), pltpu.VMEM((GROUP, 1, 128), f32),
-            pltpu.SemaphoreType.DMA((4,)), pltpu.SemaphoreType.DMA((6,)),
+            pltpu.SemaphoreType.DMA((6,)), pltpu.SemaphoreType.DMA((6,)),
         ] + [pltpu.SemaphoreType.DMA((GROUP,))] * 12,
         compiler_params=pltpu.CompilerParams(
             collective_id=0, has_side_effects=True, vmem_limit_bytes=60 << 20),
-    )(source, patch_index, visibilities, vis_weight, cell_index, tap_offsets)
+    )(patch_index, routes, visibilities, vis_weight, cell_index, tap_offsets)
 
 
 UNROLL = 64
@@ -473,17 +499,8 @@
 
 
 def shards(visibilities, vis_weight, cell_index, tap_offsets, routes, patch_index, kernel):
-    blocks = visibilities.shape[0]
-    block_ids = lax.broadcasted_iota(i32, (blocks, blocks), 0)
-    step = lax.broadcasted_iota(i32, (blocks, blocks), 1)
-    z, x, core, y = position()
-    (dz, dc), (dx, dy) = far_step(step // GROUP), near_step(step % GROUP)
-    target = ((((z + dz) % ZS) * XS + (x + dx) % XS) * CORES + (core + dc) % CORES) * YS + (y + dy) % YS
-    named = routes == target
-    first = jnp.min(jnp.where(named, block_ids, blocks), axis=0)
-    last = jnp.max(jnp.where(named, block_ids, -1), axis=0)
-    source = jnp.stack([first, jnp.where(last > first, last, blocks)])
-    far, near, patches = exchange(source, patch_index, visibilities, vis_weight, cell_index, tap_offsets)
+    far, near, patches = exchange(
+        patch_index, routes.reshape(1, BLOCKS), visibilities, vis_weight, cell_index, tap_offsets)
     tile, right, lower, corner = make_tile(
         patches, far.reshape(BLOCKS, 3, 1, 128), near.reshape(BLOCKS, 3, 1, 128), kernel.T)
     tile = finish(tile, *margins(right, lower, corner))

time: 71.5 us -> 70.2 us (0.982)
  other arithmetic: 1.44 us -> 0 us
    reduce_min x1 -> x0, other arithmetic: 0.83 us -> none  [shards(): first = jnp.min(jnp.where(named, block_ids, blocks), axis=0)]
where the time goes in v4:
time: 70.2 us; the launch traced here: 70 us
  Pallas kernels  70 us (100%)
    pallas_call x1, Pallas kernels, exchange(): pl.pallas_call(exchange_kernel, out_shape=(got, got, jax.ShapeDtypeStruct...  32.2 us
    pallas_call x1, Pallas kernels, make_tile(): pl.pallas_call(grid_kernel, out_shape=(jax.ShapeDtypeStruct((2, TILE, TIL...  25.8 us
    pallas_call x1, Pallas kernels, margins(): pl.pallas_call(margins_kernel, out_shape=tuple((jax.ShapeDtypeStruct(a.sh...  9.36 us
    pallas_call x1, Pallas kernels, finish(): pl.pallas_call(finish_kernel, out_shape=jax.ShapeDtypeStruct(tile.shape,...  2.57 us

profile of v4, /device:TPU:8, one launch (start us, length us, event | category | flops | bytes accessed | tf_op | source)
XLA Modules:
  0.0 70.0 jit_solution(9436557802095419130)
XLA Ops:
  0.0 32.2 %shard_map.73 = (f32[16,16,3,1,128]{4,3,2,1,0:T(1,128)}, f32[16,16,3,1,128]{4,3,2,1,0:T(1,128)}, s32[4,128]{1,0:T(4,128)}) custom-call(s32[256]{0:T(256)} %patch_ref.1, s32[1,256]{1,0:T(1,128)} %bitcast.8, f32[256,2,128]{2,1,0:T(2,128)} %vis_any.1, f32[256,128]{1,0:T(8,128)} %weight_any.1, s32[256,128]{1,0:T(8,128)} %cell_any.1, s32[256,128]{1,0:T(8,128)} %tap_any.1), custom_call_target="tpu_custom_call" | custom-call | tf_op jit(solution)/shard_map/pallas_call | solution.py:202
  32.2 25.8 %shard_map.74 = (f32[2,1024,1024]{2,1,0:T(8,128)}, f32[2,64,128]{2,1,0:T(8,128)}, f32[2,8,1024]{2,1,0:T(8,128)}, f32[2,8,128]{2,1,0:T(8,128)}) custom-call(s32[4,128]{1,0:T(4,128)} %get-tuple-element.15.patch_ref, f32[256,3,1,128]{3,2,1,0:T(1,128)} %bitcast.5, f32[256,3,1,128]{3,2,1,0:T(1,128)} %bitcast.6, f32[8,16]{1,0:T(8,128)} %bitcast.7), custom_call_target="tpu_custom_call" | custom-call | tf_op jit(solution)/shard_map/pallas_call | solution.py:392
  58.1 9.4 %shard_map.75 = (f32[2,64,128]{2,1,0:T(8,128)}, f32[2,8,1024]{2,1,0:T(8,128)}, f32[2,8,128]{2,1,0:T(8,128)}) custom-call(f32[2,64,128]{2,1,0:T(8,128)} %get-tuple-element.19.right_ref, f32[2,8,1024]{2,1,0:T(8,128)} %get-tuple-element.20.lower_ref, f32[2,8,128]{2,1,0:T(8,128)} %get-tuple-element.21.corner_ref), custom_call_target="tpu_custom_call" | custom-call | tf_op jit(solution)/shard_map/pallas_call | solution.py:434
  67.4 2.6 %shard_map.76 = f32[2,1024,1024]{2,1,0:T(8,128)} custom-call(f32[2,1024,1024]{2,1,0:T(8,128)} %get-tuple-element.18.tile_in, f32[2,64,128]{2,1,0:T(8,128)} %get-tuple-element.22.left_any, f32[2,8,1024]{2,1,0:T(8,128)} %get-tuple-element.23.upper_any, f32[2,8,128]{2,1,0:T(8,128)} %get-tuple-element.24.corner_any), custom_call_target="tpu_custom_call", output_to_operand_aliasing={{}: (0, {})} | custom-call | tf_op jit(solution)/shard_map/pallas_call | solution.py:487

commit v5 on v4

--- a/solution.py
+++ b/solution.py
@@ -218,7 +218,7 @@
     )(patch_index, routes, visibilities, vis_weight, cell_index, tap_offsets)
 
 
-UNROLL = 64
+UNROLL = 128
 SLOTS = 2 * BLOCKS
 ROWS = 2 * EXT
 CHUNKS = 4

time: 70.2 us -> 69.1 us (0.984)
  Pallas kernels: 70 us -> 68.9 us
    pallas_call x1, Pallas kernels: 25.8 us -> 24.8 us  [make_tile(): pl.pallas_call(grid_kernel, out_shape=(jax.ShapeDtypeStruct((2, TILE, TIL...]
where the time goes in v5:
time: 69.1 us; the launch traced here: 69 us
  Pallas kernels  68.9 us (100%)
    pallas_call x1, Pallas kernels, exchange(): pl.pallas_call(exchange_kernel, out_shape=(got, got, jax.ShapeDtypeStruct...  32.2 us
    pallas_call x1, Pallas kernels, make_tile(): pl.pallas_call(grid_kernel, out_shape=(jax.ShapeDtypeStruct((2, TILE, TIL...  24.8 us
    pallas_call x1, Pallas kernels, margins(): pl.pallas_call(margins_kernel, out_shape=tuple((jax.ShapeDtypeStruct(a.sh...  9.36 us
    pallas_call x1, Pallas kernels, finish(): pl.pallas_call(finish_kernel, out_shape=jax.ShapeDtypeStruct(tile.shape,...  2.57 us

profile of v5, /device:TPU:8, one launch (start us, length us, event | category | flops | bytes accessed | tf_op | source)
XLA Modules:
  0.0 69.0 jit_solution(6932152321456942471)
XLA Ops:
  0.0 32.2 %shard_map.73 = (f32[16,16,3,1,128]{4,3,2,1,0:T(1,128)}, f32[16,16,3,1,128]{4,3,2,1,0:T(1,128)}, s32[4,128]{1,0:T(4,128)}) custom-call(s32[256]{0:T(256)} %patch_ref.1, s32[1,256]{1,0:T(1,128)} %bitcast.8, f32[256,2,128]{2,1,0:T(2,128)} %vis_any.1, f32[256,128]{1,0:T(8,128)} %weight_any.1, s32[256,128]{1,0:T(8,128)} %cell_any.1, s32[256,128]{1,0:T(8,128)} %tap_any.1), custom_call_target="tpu_custom_call" | custom-call | tf_op jit(solution)/shard_map/pallas_call | solution.py:202
  32.2 24.8 %shard_map.74 = (f32[2,1024,1024]{2,1,0:T(8,128)}, f32[2,64,128]{2,1,0:T(8,128)}, f32[2,8,1024]{2,1,0:T(8,128)}, f32[2,8,128]{2,1,0:T(8,128)}) custom-call(s32[4,128]{1,0:T(4,128)} %get-tuple-element.15.patch_ref, f32[256,3,1,128]{3,2,1,0:T(1,128)} %bitcast.5, f32[256,3,1,128]{3,2,1,0:T(1,128)} %bitcast.6, f32[8,16]{1,0:T(8,128)} %bitcast.7), custom_call_target="tpu_custom_call" | custom-call | tf_op jit(solution)/shard_map/pallas_call | solution.py:392
  57.0 9.4 %shard_map.75 = (f32[2,64,128]{2,1,0:T(8,128)}, f32[2,8,1024]{2,1,0:T(8,128)}, f32[2,8,128]{2,1,0:T(8,128)}) custom-call(f32[2,64,128]{2,1,0:T(8,128)} %get-tuple-element.19.right_ref, f32[2,8,1024]{2,1,0:T(8,128)} %get-tuple-element.20.lower_ref, f32[2,8,128]{2,1,0:T(8,128)} %get-tuple-element.21.corner_ref), custom_call_target="tpu_custom_call" | custom-call | tf_op jit(solution)/shard_map/pallas_call | solution.py:434
  66.4 2.6 %shard_map.76 = f32[2,1024,1024]{2,1,0:T(8,128)} custom-call(f32[2,1024,1024]{2,1,0:T(8,128)} %get-tuple-element.18.tile_in, f32[2,64,128]{2,1,0:T(8,128)} %get-tuple-element.22.left_any, f32[2,8,1024]{2,1,0:T(8,128)} %get-tuple-element.23.upper_any, f32[2,8,128]{2,1,0:T(8,128)} %get-tuple-element.24.corner_any), custom_call_target="tpu_custom_call", output_to_operand_aliasing={{}: (0, {})} | custom-call | tf_op jit(solution)/shard_map/pallas_call | solution.py:487
